TPU v7x, 32 devices: a whole 2x2x4 slice. The times are simulated.
32 devices in a mesh: ens: 2 (over x), col: 16 (over z, y, core).
Axes of the slice: x: 2, y: 2, z: 4, core: 2. Of those that a mesh axis runs over, the one named last changes fastest.
Arguments:
- gcm_state: float32 [4608, 128], P(('ens', 'col')), parts along dimension 0, may hold values from -6 to 6
- cloud_model_state: bfloat16 [9216, 32, 128], P(('ens', 'col')), parts along dimension 0, may hold values from -6 to 6
- owner: int32 [4608, 1], P(('ens', 'col')), parts along dimension 0, may hold values from 0 to 15; in each aligned block of 144 rows (0 to 143, 144 to 287, ...) at most 18 rows name the same one
- substeps: int32 [4608], P(('ens', 'col')), parts along dimension 0, may hold values from 1 to 2
- neighbours: int32 [512, 4], P(('ens', 'col')), parts along dimension 0, may hold values from 0 to 255, as said below
- mig_slot: int32 [4096], P(('ens', 'col')), parts along dimension 0, may hold values from 0 to 287, as said below
- mig_dest: int32 [4096, 1], P(('ens', 'col')), parts along dimension 0, may hold values from 0 to 15; in each aligned block of 128 rows (0 to 127, 128 to 255, ...) at most 16 rows name the same one
Outputs:
- gcm_new: float32 [4608, 128], P(('ens', 'col')), parts along dimension 0
- crm_new: bfloat16 [9216, 32, 128], P(('ens', 'col')), parts along dimension 0
- arrived: bfloat16 [8192, 32, 128], P(('ens', 'col')), parts along dimension 0
There are 2 independent parts, one for each index of `ens`. A program takes and returns all parts, laid end to end along the dimension named above; each array names one. Nothing has to cross between parts.
Inputs may be any that keep to these rules, and one draw needn't show every extreme that they name: The 144 columns of one device name each owner at most 18 times. `mig_dest`: the 128 migrations of one device name each destination at most 16 times. `mig_slot`: the 128 slots listed by one device are distinct. neighbours 0 and 1 of element e lie 1 to 8 elements before e in Morton order and neighbours 2 and 3 1 to 8 after it, cyclically over 256; for every e that is a multiple of 16, neighbour 0 of e is exactly 8 before it and neighbour 3 of e + 15 exactly 8 after that one.
All inputs are finite; a program needn't handle non-finite values.
Results may differ from a plain program's by a relative error of at most 0.0033.
Values may be sent and summed in bfloat16 or wider, within the bound.
A program may use at most 128 MiB of HBM per device.

v0:
```python
import jax
import jax.numpy as jnp
from jax import lax
from jax.sharding import PartitionSpec as P

SUBMAX = 2


EDGE_RATE = 0.2
ACROSS_RATE = 0.2
VERTICAL_RATE = 0.15
NUDGE_RATE = 0.3
PHASE_RATE = 0.25


def with_halo(block, sides, width):
    for axis, dim in sides:
        count = lax.axis_size(axis)
        forward = [(i, i + 1) for i in range(count - 1)]
        forward.append((count - 1, 0))
        backward = [(target, source) for source, target in forward]
        low = lax.ppermute(
            lax.slice_in_dim(block, block.shape[dim] - width, None, axis=dim), axis, forward
        )
        high = lax.ppermute(lax.slice_in_dim(block, 0, width, axis=dim), axis, backward)
        block = jnp.concatenate([low, block, high], axis=dim)
    return block


def ranks(targets, model_width):
    hits = (targets[:, None] == jnp.arange(model_width, dtype=jnp.int32)[None, :]).astype(jnp.int32)
    before = jnp.cumsum(hits, axis=0) - hits
    return jnp.sum(before * hits, axis=1)


def crm_steps(column_state, forcing, counts):
    slot_number, across_flux, model_width = column_state.shape
    level_count = model_width // 2
    state_field = column_state.astype(jnp.float32)
    anchor = jnp.mean(state_field, axis=1)
    signs = jnp.array([1.0, -1.0], jnp.float32)[None, None, :, None]
    for step in range(SUBMAX):
        beside = (
            jnp.roll(state_field, 1, axis=1) + jnp.roll(state_field, -1, axis=1) - 2.0 * state_field
        )
        split_point = state_field.reshape(slot_number, across_flux, 2, level_count)
        padded = jnp.pad(split_point, ((0, 0), (0, 0), (0, 0), (1, 1)), mode="edge")
        vertical_flux = (padded[..., 2:] + padded[..., :-2] - 2.0 * split_point).reshape(
            slot_number, across_flux, model_width
        )
        phase = PHASE_RATE * jnp.tanh(split_point[:, :, 1, :] - 0.5 * split_point[:, :, 0, :])
        phases = (phase[:, :, None, :] * signs).reshape(slot_number, across_flux, model_width)
        average = jnp.mean(state_field, axis=1, keepdims=True)
        moved = (
            state_field
            + ACROSS_RATE * beside
            + VERTICAL_RATE * vertical_flux
            + NUDGE_RATE * (forcing[:, None, :] - average)
            + phases
        )
        active = (step < counts)[:, None, None]
        state_field = jnp.where(active, moved, state_field)
    divisor = jnp.maximum(counts, 1).astype(jnp.float32)[:, None]
    tendency = (jnp.mean(state_field, axis=1) - anchor) / divisor
    return (state_field.astype(jnp.bfloat16), tendency)


def per_device(gcm_state, cloud_model_state, owner, substeps, neighbours, mig_slot, mig_dest):
    device_count = lax.axis_size("col")
    device_index = lax.axis_index("col")
    columns, model_width = gcm_state.shape
    elements = columns // 9
    margin = elements // 2
    slot_total, across_flux = (cloud_model_state.shape[0], cloud_model_state.shape[1])
    slot_capacity = slot_total // device_count
    listed = mig_slot.shape[0]
    move_cap = max(2, 2 * listed // device_count)
    move_dest = mig_dest[:, 0]
    move_place = move_dest * move_cap + ranks(move_dest, device_count)
    means = jnp.mean(gcm_state.reshape(elements, 9, model_width), axis=1)
    extended = with_halo(means, (("col", 0),), margin)
    local_ids = jnp.mod(neighbours - device_index * elements + margin, elements * device_count)
    beside_all = jnp.sum(extended[local_ids], axis=1)
    dynamic_state = gcm_state + jnp.repeat(EDGE_RATE * (beside_all - 4.0 * means), 9, axis=0)
    target = owner[:, 0]
    placed_slots = target * slot_capacity + ranks(target, device_count)
    outgoing_rows = (
        jnp.zeros((slot_total, model_width), jnp.float32).at[placed_slots].set(dynamic_state)
    )
    send_count_table = (
        jnp.zeros((slot_total,), jnp.float32).at[placed_slots].set(substeps.astype(jnp.float32))
    )
    forcing, got_counts = (
        lax.all_to_all(
            outgoing_rows.astype(jnp.bfloat16), "col", split_axis=0, concat_axis=0, tiled=True
        ).astype(outgoing_rows.dtype),
        lax.all_to_all(
            send_count_table.astype(jnp.bfloat16), "col", split_axis=0, concat_axis=0, tiled=True
        ).astype(send_count_table.dtype),
    )
    after, tendency = crm_steps(cloud_model_state, forcing, got_counts.astype(jnp.int32))
    crm_new = after.at[mig_slot].set(jnp.zeros((across_flux, model_width), jnp.bfloat16))
    returned = lax.all_to_all(
        tendency.astype(jnp.bfloat16), "col", split_axis=0, concat_axis=0, tiled=True
    ).astype(tendency.dtype)
    departing = (
        jnp.zeros((device_count * move_cap, across_flux, model_width), jnp.bfloat16)
        .at[move_place]
        .set(after[mig_slot])
    )
    arrived = lax.all_to_all(departing, "col", split_axis=0, concat_axis=0, tiled=True)
    gcm_new = dynamic_state + returned[placed_slots]
    return (gcm_new, crm_new, arrived)


def solution(mesh):
    in_specs = (
        P(("ens", "col"), None),
        P(("ens", "col"), None, None),
        P(("ens", "col"), None),
        P(("ens", "col")),
        P(("ens", "col"), None),
        P(("ens", "col")),
        P(("ens", "col"), None),
    )
    out_specs = (
        P(("ens", "col"), None),
        P(("ens", "col"), None, None),
        P(("ens", "col"), None, None),
    )
    return jax.shard_map(
        per_device, mesh=mesh, in_specs=in_specs, out_specs=out_specs, check_vma=False
    )
```

profile of v0, /device:TPU:15, one launch (start us, length us, event | category | flops | bytes accessed | tf_op | source)
XLA Modules:
  0.0 223.0 jit_solution(9537356946038865858)
XLA Ops:
  8.9 6.6 %all-to-all-start = ((bf16[16,18,1]{1,2,0:T(2,128)(2,1)}), bf16[16,18,1]{1,2,0:T(2,128)(2,1)S(1)}, u32[]{:S(2)}, u32[]{:S(2)}) async-start(bf16[16,18,1]{1,2,0:T(2,128)(2,1)} %all_to_all.25), calls=%async_computation | async-start | bytes 16384 | tf_op jit(solution)/shard_map/all_to_all | solution.py:97
  18.1 5.7 %copy.34 = f32[288,32,128]{0,2,1:T(8,128)} copy(bf16[288,32,128]{2,1,0:T(8,128)(2,1)} %param.9) | data formatting | bytes 7077888 | tf_op jit(solution)/shard_map/convert_element_type | solution.py:39
  25.3 5.3 %fusion.27 = f32[288,32,64]{0,2,1:T(8,128)} fusion(f32[288,32,2,64]{0,3,2,1:T(8,128)} %bitcast.37), kind=kLoop, calls=%fused_computation.42 | loop fusion | flops 1769472 | bytes 7077888 | tf_op jit(solution)/shard_map/mul | solution.py:52
  30.7 5.6 %fusion.46 = (f32[288,31,128]{2,1,0:T(8,128)}, f32[288,31,128]{2,1,0:T(8,128)}) fusion(bf16[288,32,128]{2,1,0:T(8,128)(2,1)S(1)} %copy-done), kind=kLoop, calls=%fused_computation.91 | loop fusion | bytes 18284544 | tf_op jit(solution)/shard_map/jit(_roll_static)/slice | solution.py:44
  37.1 10.3 %fusion.5 = f32[288,32,2,64]{0,3,2,1:T(8,128)} fusion(f32[288,32,2,64]{0,3,2,1:T(8,128)} %bitcast.38, f32[288,32,2,1]{0,3,2,1:T(1,128)S(1)} %get-tuple-element.12, f32[288,32,2,1]{0,3,2,1:T(1,128)S(1)} %get-tuple-element.11), kind=kLoop, calls=%fused_computation.15 | loop fusion | flops 7077888 | bytes 9584640 | tf_op jit(solution)/shard_map/mul | solution.py:57
  47.4 6.3 %copy.35 = f32[288,32,128]{2,1,0:T(8,128)} copy(f32[288,32,128]{0,2,1:T(8,128)} %bitcast.44) | data formatting | bytes 9437184 | tf_op jit(solution)/shard_map/mul | solution.py:57
  53.7 5.3 %mul.152 = f32[288,32,2,64]{0,3,2,1:T(8,128)} broadcast(f32[288,32,64]{0,2,1:T(8,128)} %fusion.27), dimensions={0,1,3} | broadcast | bytes 7077888 | tf_op jit(solution)/shard_map/mul | solution.py:52
  58.9 6.3 %copy.36 = f32[288,32,128]{2,1,0:T(8,128)} copy(f32[288,32,128]{0,2,1:T(8,128)} %bitcast.46) | data formatting | bytes 9437184 | tf_op jit(solution)/shard_map/mul | solution.py:52
  68.0 6.1 %all-to-all-start.1 = ((bf16[16,18,128]{2,1,0:T(8,128)(2,1)}), bf16[16,18,128]{2,1,0:T(8,128)(2,1)S(1)}, u32[]{:S(2)}, u32[]{:S(2)}) async-start(bf16[16,18,128]{2,1,0:T(8,128)(2,1)} %all_to_all.21), calls=%async_computation.1 | async-start | bytes 196608 | tf_op jit(solution)/shard_map/all_to_all | solution.py:94
  74.1 4.7 %all-to-all-done.1 = bf16[16,18,128]{2,1,0:T(8,128)(2,1)S(1)} async-done(((bf16[16,18,128]{2,1,0:T(8,128)(2,1)}), bf16[16,18,128]{2,1,0:T(8,128)(2,1)S(1)}, u32[]{:S(2)}, u32[]{:S(2)}) %all-to-all-start.1) | async-done | bytes 73760 | tf_op jit(solution)/shard_map/all_to_all | solution.py:94
  78.9 10.4 %fusion.39 = (f32[288,128]{1,0:T(8,128)}, f32[288,32,128]{2,1,0:T(8,128)}) fusion(f32[288,32,128]{2,1,0:T(8,128)} %copy.36, f32[128]{0:T(128)S(1)} %mul.155, f32[288,128]{1,0:T(8,128)S(1)} %subtract_multiply_fusion.1, f32[288,32,128]{2,1,0:T(8,128)} %copy.35, f32[288,1,128]{2,1,0:T(1,128)S(1)} %get-tuple-element.18, f32[288,31,128]{2,1,0:T(8,128)} %get-tuple-element.20, ...), kind=kLoop, calls=%fused_computation.85 | loop fusion | flops 16478208 | bytes 26247968 | tf_op jit(solution)/shard_map/reduce_sum | solution.py:53
  89.3 6.2 %copy.37 = f32[288,32,128]{0,2,1:T(8,128)} copy(f32[288,32,128]{2,1,0:T(8,128)} %get-tuple-element.8) | data formatting | bytes 9437184 | tf_op jit(solution)/shard_map/jit(_where)/select_n | solution.py:62
  97.2 3.6 %fusion.23 = f32[288,32,64]{0,2,1:T(8,128)S(1)} fusion(f32[288,32,2,64]{0,3,2,1:T(8,128)} %bitcast.40), kind=kLoop, calls=%fused_computation.37 | loop fusion | flops 1769472 | bytes 7077888 | tf_op jit(solution)/shard_map/mul | solution.py:52
  100.8 4.9 %fusion.44 = (f32[288,31,128]{2,1,0:T(8,128)}, f32[288,31,128]{2,1,0:T(8,128)}) fusion(f32[288,32,128]{2,1,0:T(8,128)S(1)} %bitcast.35), kind=kLoop, calls=%fused_computation.89 | loop fusion | bytes 18284544 | tf_op jit(solution)/shard_map/jit(_roll_static)/slice | solution.py:44
  106.6 4.1 %fusion.2 = f32[288,32,2,64]{0,3,2,1:T(8,128)} fusion(f32[288,32,2,64]{0,3,2,1:T(8,128)S(1)} %bitcast.43, f32[288,32,2,1]{0,3,2,1:T(1,128)S(1)} %get-tuple-element.10, f32[288,32,2,1]{0,3,2,1:T(1,128)S(1)} %get-tuple-element.9), kind=kLoop, calls=%fused_computation.10 | loop fusion | flops 7077888 | bytes 9584640 | tf_op jit(solution)/shard_map/mul | solution.py:57
  110.7 6.3 %copy.38 = f32[288,32,128]{2,1,0:T(8,128)} copy(f32[288,32,128]{0,2,1:T(8,128)} %bitcast.45) | data formatting | bytes 9437184 | tf_op jit(solution)/shard_map/mul | solution.py:57
  118.6 3.4 %mul.167 = f32[288,32,2,64]{0,3,2,1:T(8,128)} broadcast(f32[288,32,64]{0,2,1:T(8,128)S(1)} %fusion.23), dimensions={0,1,3} | broadcast | bytes 7077888 | tf_op jit(solution)/shard_map/mul | solution.py:52
  122.0 6.3 %copy.39 = f32[288,32,128]{2,1,0:T(8,128)} copy(f32[288,32,128]{0,2,1:T(8,128)} %bitcast.47) | data formatting | bytes 9437184 | tf_op jit(solution)/shard_map/mul | solution.py:52
  128.3 11.6 %fusion.37 = (bf16[288,32,128]{2,1,0:T(8,128)(2,1)S(1)}, f32[288,32,128]{2,1,0:T(8,128)}) fusion(f32[288,32,128]{2,1,0:T(8,128)} %get-tuple-element.8, f32[288,32,128]{2,1,0:T(8,128)} %copy.39, f32[128]{0:T(128)S(1)} %mul.155, f32[288,128]{1,0:T(8,128)S(1)} %copy-done.2, f32[288,32,128]{2,1,0:T(8,128)} %copy.38, f32[288,1,128]{2,1,0:T(1,128)S(1)} %copy-done.4, ...), kind=kLoop, calls=%fused_computation.84 | loop fusion | flops 15335424 | bytes 30819104 | tf_op jit(solution)/shard_map/convert_element_type | solution.py:65
  143.9 6.2 %all-to-all-start.2 = ((bf16[16,18,128]{2,1,0:T(8,128)(2,1)}), bf16[16,18,128]{2,1,0:T(8,128)(2,1)S(1)}, u32[]{:S(2)}, u32[]{:S(2)}) async-start(bf16[16,18,128]{2,1,0:T(8,128)(2,1)} %divide_convert_fusion), calls=%async_computation.2 | async-start | bytes 196608 | tf_op jit(solution)/shard_map/all_to_all | solution.py:103
  152.4 13.7 %scatter_fusion.1 = bf16[256,32,128]{2,1,0:T(8,128)(2,1)} fusion(bf16[256,32,128]{2,1,0:T(8,128)(2,1)} %broadcast_in_dim.55, s32[128]{0:T(128)S(1)} %fusion.36, bf16[128,32,128]{2,1,0:T(8,128)(2,1)S(1)} %gather_fusion.2), kind=kCustom, calls=%fused_computation.6 | custom fusion | bytes 3146240 | tf_op jit(solution)/shard_map/scatter | solution.py:109
  166.1 6.1 %all-to-all-start.3 = ((bf16[256,32,128]{2,1,0:T(8,128)(2,1)}), bf16[256,32,128]{2,1,0:T(8,128)(2,1)}, u32[]{:S(2)}, u32[]{:S(2)}) async-start(bf16[256,32,128]{2,1,0:T(8,128)(2,1)} %scatter_fusion.1), calls=%async_computation.3 | async-start | bytes 4194304 | tf_op jit(solution)/shard_map/all_to_all | solution.py:111
  172.4 4.5 %scatter_fusion = bf16[288,32,128]{2,1,0:T(8,128)(2,1)S(1)} fusion(bf16[288,32,128]{2,1,0:T(8,128)(2,1)S(1)} %get-tuple-element.5, s32[128]{0:T(128)S(1)} %compare_select_fusion.3, bf16[128,32,128]{2,1,0:T(8,128)(2,1)S(1)} %broadcast.151), kind=kCustom, calls=%fused_computation.5 | custom fusion | bytes 3146240 | tf_op jit(solution)/shard_map/scatter | solution.py:102
  179.1 40.6 %all-to-all-done.3 = bf16[256,32,128]{2,1,0:T(8,128)(2,1)} async-done(((bf16[256,32,128]{2,1,0:T(8,128)(2,1)}), bf16[256,32,128]{2,1,0:T(8,128)(2,1)}, u32[]{:S(2)}, u32[]{:S(2)}) %all-to-all-start.3) | async-done | bytes 2097184 | tf_op jit(solution)/shard_map/all_to_all | solution.py:111
  (101 shorter events, 32.1 us)
Async XLA Ops:
  1.6 64.1 %collective-permute-start = (f32[8,128]{1,0:T(8,128)S(1)}, f32[8,128]{1,0:T(8,128)S(1)}, u32[]{:S(2)}, u32[]{:S(2)}) collective-permute-start(f32[8,128]{1,0:T(8,128)S(1)} %get-tuple-element.21), channel_id=1, source_target_pairs={{0,1},{1,2},{2,3},{3,4},{4,5},{5,6},{6,7},{7,8},{8,9},{9,10},{10,1... | collective-permute-start | bytes 12296 | tf_op jit(solution)/shard_map/ppermute | solution.py:22
  3.4 62.2 %collective-permute-start.1 = (f32[8,128]{1,0:T(8,128)S(1)}, f32[8,128]{1,0:T(8,128)S(1)}, u32[]{:S(2)}, u32[]{:S(2)}) collective-permute-start(f32[8,128]{1,0:T(8,128)S(1)} %get-tuple-element.22), channel_id=1, source_target_pairs={{1,0},{2,1},{3,2},{4,3},{5,4},{6,5},{7,6},{8,7},{9,8},{10,9},{11,1... | collective-permute-start | bytes 12296 | tf_op jit(solution)/shard_map/ppermute | solution.py:25
  8.9 56.5 %all-to-all-start = ((bf16[16,18,1]{1,2,0:T(2,128)(2,1)}), bf16[16,18,1]{1,2,0:T(2,128)(2,1)S(1)}, u32[]{:S(2)}, u32[]{:S(2)}) async-start(bf16[16,18,1]{1,2,0:T(2,128)(2,1)} %all_to_all.25), calls=%async_computation | async-start | bytes 16384 | tf_op jit(solution)/shard_map/all_to_all | solution.py:97
  25.3 5.4 %copy-start = (bf16[288,32,128]{2,1,0:T(8,128)(2,1)S(1)}, bf16[288,32,128]{2,1,0:T(8,128)(2,1)}, u32[]{:S(2)}) copy-start(bf16[288,32,128]{2,1,0:T(8,128)(2,1)} %param.9) | copy-start | bytes 7077892
  30.7 5.8 %copy-start.8 = (s32[16,4]{0,1:T(4,128)S(1)}, s32[16,4]{0,1:T(4,128)}, u32[]{:S(2)}) copy-start(s32[16,4]{0,1:T(4,128)} %param.12) | copy-start | bytes 772
  30.7 6.0 %copy-start.7 = (s32[128,1]{0,1:T(1,128)S(1)}, s32[128,1]{0,1:T(1,128)}, u32[]{:S(2)}) copy-start(s32[128,1]{0,1:T(1,128)} %param.14) | copy-start | bytes 1540
  58.9 6.3 %copy-start.10 = (f32[2]{0:T(128)S(1)}, f32[2]{0:T(128)}, u32[]{:S(2)}) copy-start(f32[2]{0:T(128)} %constant.85.clone) | copy-start | bytes 28
  58.9 7.4 %copy-start.5 = (f32[144,128]{1,0:T(8,128)S(1)}, f32[144,128]{1,0:T(8,128)}, u32[]{:S(2)}) copy-start(f32[144,128]{1,0:T(8,128)} %param.8) | copy-start | bytes 221188
  66.4 22.9 %copy-start.6 = (f32[144,128]{1,0:T(8,128)}, f32[144,128]{1,0:T(8,128)S(1)}, u32[]{:S(2)}) copy-start(f32[144,128]{1,0:T(8,128)S(1)} %add.100) | copy-start | bytes 221188
  68.0 10.8 %all-to-all-start.1 = ((bf16[16,18,128]{2,1,0:T(8,128)(2,1)}), bf16[16,18,128]{2,1,0:T(8,128)(2,1)S(1)}, u32[]{:S(2)}, u32[]{:S(2)}) async-start(bf16[16,18,128]{2,1,0:T(8,128)(2,1)} %all_to_all.21), calls=%async_computation.1 | async-start | bytes 196608 | tf_op jit(solution)/shard_map/all_to_all | solution.py:94
  95.5 5.3 %slice-start = ((s8[4718592]{0:T(1024)(128)(4,1)}), s8[4194304]{0:T(1024)(128)(4,1)S(1)}, s32[]{:S(2)}) async-start(s8[4718592]{0:T(1024)(128)(4,1)} %bitcast.34), calls=%async_computation.4 | async-start | bytes 8388608
  97.2 3.6 %slice-start.1 = ((s8[4718592]{0:T(1024)(128)(4,1)}), s8[524288]{0:T(1024)(128)(4,1)S(1)}, s32[]{:S(2)}) async-start(s8[4718592]{0:T(1024)(128)(4,1)} %bitcast.34), calls=%async_computation.5 | async-start | bytes 1048576
  97.2 9.4 %slice-start.2 = ((s8[6291456]{0:T(1024)(128)(4,1)}), s8[4194304]{0:T(1024)(128)(4,1)S(1)}, s32[]{:S(2)}) async-start(s8[6291456]{0:T(1024)(128)(4,1)} %bitcast.41), calls=%async_computation.6 | async-start | bytes 8388608
  100.8 5.8 %slice-start.3 = ((s8[6291456]{0:T(1024)(128)(4,1)}), s8[2097152]{0:T(1024)(128)(4,1)S(1)}, s32[]{:S(2)}) async-start(s8[6291456]{0:T(1024)(128)(4,1)} %bitcast.41), calls=%async_computation.7 | async-start | bytes 4194304
  122.0 6.3 %copy-start.2 = (f32[288,128]{1,0:T(8,128)S(1)}, f32[288,128]{1,0:T(8,128)}, u32[]{:S(2)}) copy-start(f32[288,128]{1,0:T(8,128)} %subtract_multiply_fusion) | copy-start | bytes 442372
  122.0 6.3 %copy-start.3 = (f32[288,1,128]{2,1,0:T(1,128)S(1)}, f32[288,1,128]{2,1,0:T(1,128)}, u32[]{:S(2)}) copy-start(f32[288,1,128]{2,1,0:T(1,128)} %get-tuple-element.13) | copy-start | bytes 442372
  122.0 6.3 %copy-start.4 = (f32[288,1,128]{2,1,0:T(1,128)S(1)}, f32[288,1,128]{2,1,0:T(1,128)}, u32[]{:S(2)}) copy-start(f32[288,1,128]{2,1,0:T(1,128)} %get-tuple-element.14) | copy-start | bytes 442372
  139.9 10.1 %copy-start.9 = (s32[128]{0:T(128)S(1)}, s32[128]{0:T(128)}, u32[]{:S(2)}) copy-start(s32[128]{0:T(128)} %param.13) | copy-start | bytes 1540
  143.9 22.3 %all-to-all-start.2 = ((bf16[16,18,128]{2,1,0:T(8,128)(2,1)}), bf16[16,18,128]{2,1,0:T(8,128)(2,1)S(1)}, u32[]{:S(2)}, u32[]{:S(2)}) async-start(bf16[16,18,128]{2,1,0:T(8,128)(2,1)} %divide_convert_fusion), calls=%async_computation.2 | async-start | bytes 196608 | tf_op jit(solution)/shard_map/all_to_all | solution.py:103
  166.1 53.6 %all-to-all-start.3 = ((bf16[256,32,128]{2,1,0:T(8,128)(2,1)}), bf16[256,32,128]{2,1,0:T(8,128)(2,1)}, u32[]{:S(2)}, u32[]{:S(2)}) async-start(bf16[256,32,128]{2,1,0:T(8,128)(2,1)} %scatter_fusion.1), calls=%async_computation.3 | async-start | bytes 4194304 | tf_op jit(solution)/shard_map/all_to_all | solution.py:111
  176.8 46.2 %copy-start.1 = (bf16[288,32,128]{2,1,0:T(8,128)(2,1)}, bf16[288,32,128]{2,1,0:T(8,128)(2,1)S(1)}, u32[]{:S(2)}) copy-start(bf16[288,32,128]{2,1,0:T(8,128)(2,1)S(1)} %scatter_fusion) | copy-start | bytes 7077892
where the time goes:
time: 225 us; the launch traced here: 223 us
  local copies, waits for them, and re-layouts  90.8 us (40%)
  other arithmetic  59.2 us (26%)
  waiting for transfers between devices  45.3 us (20%)
  starting transfers between devices  26.8 us (12%)
    all_to_all x1, waiting for transfers between devices, per_device(): lax.all_to_all(departing, 'col', split_axis=0, concat_axis=0, tiled=True)  40.6 us
    mul x6, local copies, waits for them, and re-layouts, crm_steps(): phase[:, :, None, :] * signs  21.4 us
    mul x2, other arithmetic, crm_steps(): VERTICAL_RATE * vertical_flux  14.4 us
    scatter x1, local copies, waits for them, and re-layouts, per_device(): departing = jnp.zeros((device_count * move_cap, across_flux, model_width)...  13.7 us
    reduce_sum x2, other arithmetic, crm_steps(): average = jnp.mean(state_field, axis=1, keepdims=True)  13 us
    mul x2, local copies, waits for them, and re-layouts, crm_steps(): VERTICAL_RATE * vertical_flux  12.5 us
    convert_element_type x1, other arithmetic, crm_steps(): return (state_field.astype(jnp.bfloat16), tendency)  11.6 us
    slice x4, local copies, waits for them, and re-layouts, crm_steps(): jnp.roll(state_field, 1, axis=1) + jnp.roll(state_field, -1, axis=1)  11.6 us
  transfers between devices with their start and end apart: 6, of which 2 were waited for; matrix products, arithmetic and copies ran while one was open for 35% of the time, Pallas kernels for 0%

commit v1 on v0

v1 whole, which is shorter than its diff:
```python
import functools

import jax
import jax.numpy as jnp
from jax import lax
from jax.experimental import pallas as pl
from jax.experimental.pallas import tpu as pltpu
from jax.sharding import PartitionSpec as P

F32, BF16, I32 = jnp.float32, jnp.bfloat16, jnp.int32
MESH = pl.DeviceIdType.MESH
GROUP = 8


def iota(shape, dim):
    return lax.broadcasted_iota(I32, shape, dim)


def ones_where(condition, dtype=BF16):
    return jnp.where(condition, 1.0, 0.0).astype(dtype)


def exact(a, b):
    return jnp.dot(a, b, preferred_element_type=F32, precision=lax.Precision.HIGHEST)


def fast(a, b):
    return jnp.dot(a, b, preferred_element_type=F32)


def step_matrices(across, width):
    size = GROUP * across
    shift = across.bit_length() - 1
    row, col = iota((size, size), 0), iota((size, size), 1)
    same = (row >> shift) == (col >> shift)
    gap = (row - col) & (across - 1)
    beside = jnp.where((gap == 1) | (gap == across - 1), 1.0, 0.0)
    middle = jnp.where(gap == 0, 3.0, 0.0)
    left = jnp.where(same, beside + middle - 1.5 / across, 0.0).astype(BF16)
    half = width // 2
    source, level = iota((width, 2 * width), 0), iota((width, 2 * width), 1)
    inside = (source < half) == (level < half)
    near = jnp.where(jnp.abs(source - level) == 1, 0.75, 0.0)
    edge = (level == 0) | (level == half - 1) | (level == half) | (level == width - 1)
    near = near - jnp.where(source == level, jnp.where(edge, 0.75, 1.5), 0.0)
    vertical = jnp.where(inside, near, 0.0)
    target = level - width
    sign = jnp.where(target < half, 1.0, -1.0)
    of_level = (source & (half - 1)) == (target & (half - 1))
    phase = jnp.where(of_level, jnp.where(source < half, -0.5, 1.0) * sign, 0.0)
    right = jnp.where(level < width, vertical, phase).astype(BF16)
    rows = iota((GROUP, size), 0)
    total = ones_where(rows == (iota((GROUP, size), 1) >> shift))
    return left, right, total


def one_step(state, forcing, left, right, across, width):
    linear = fast(left, state)
    levels = fast(state, right)
    pushed = jnp.broadcast_to((1.5 * forcing)[:, None, :], (GROUP, across, width))
    pushed = pushed.reshape(GROUP * across, width)
    return 0.2 * (linear + levels[:, :width] + pushed) + 0.25 * jnp.tanh(levels[:, width:])


def kernel(n, cap, capp, mcap,
           gcm_ref, cloud_ref, owner_col_ref, owner_row_ref, substeps_ref, neigh_ref,
           mig_row_ref, pick_ref,
           new_ref, crm_ref, arrived_ref,
           ext, dyn, fsend, frecv, fc, keep, tend, tsend, trecv, after, depart,
           halo_send, halo_recv, f_send, f_recv, t_send, t_recv, m_send, m_recv, own_sem):
    me = lax.axis_index("col")
    cols, width = gcm_ref.shape
    slots, across, _ = cloud_ref.shape
    elements = cols // 9
    margin = elements // 2
    table = n * capp
    shift = capp.bit_length() - 1
    right_dev, left_dev = lax.rem(me + 1, n), lax.rem(me + n - 1, n)

    barrier = pltpu.get_barrier_semaphore()

    def greet(k, carry):
        pl.semaphore_signal(barrier, inc=1, device_id={"col": lax.rem(me + k, n)}, device_id_type=MESH)
        return carry

    lax.fori_loop(1, n, greet, 0)

    gcm = gcm_ref[...]
    place = iota((elements, cols), 1) - 9 * iota((elements, cols), 0)
    member = ones_where((place >= 0) & (place < 9), F32)
    means = exact(member, gcm) * (1.0 / 9.0)
    ext[pl.ds(margin, elements), :] = means
    pl.semaphore_wait(barrier, n - 1)

    up = pltpu.make_async_remote_copy(
        src_ref=ext.at[pl.ds(elements, margin)], dst_ref=ext.at[pl.ds(0, margin)],
        send_sem=halo_send.at[0], recv_sem=halo_recv.at[0],
        device_id={"col": right_dev}, device_id_type=MESH)
    down = pltpu.make_async_remote_copy(
        src_ref=ext.at[pl.ds(margin, margin)], dst_ref=ext.at[pl.ds(margin + elements, margin)],
        send_sem=halo_send.at[1], recv_sem=halo_recv.at[1],
        device_id={"col": left_dev}, device_id_type=MESH)
    up.start()
    down.start()

    owner_row = owner_row_ref[...]
    hits = iota((n, cols), 0) == owner_row
    earlier = ones_where(iota((cols, cols), 0) < iota((cols, cols), 1))
    before = fast(ones_where(hits), earlier)
    rank = jnp.sum(jnp.where(hits, before, 0.0), axis=0, keepdims=True).astype(I32)
    place_row = owner_row * capp + rank
    scatter = ones_where(iota((table, cols), 0) == place_row)
    gone = iota((slots, mig_row_ref.shape[1]), 0) == mig_row_ref[...]
    gone = jnp.max(jnp.where(gone, 1.0, 0.0), axis=1, keepdims=True)
    keep[...] = jnp.broadcast_to(1.0 - gone, (slots, width))
    after[pl.ds(slots, 1)] = jnp.zeros((1, across, width), BF16)

    ids = neigh_ref[...] - me * elements + margin
    span = elements * n
    ids = jnp.where(ids < 0, ids + span, ids)
    ids = jnp.where(ids >= span, ids - span, ids)
    wide = iota((elements, elements + 2 * margin), 1)
    weights = jnp.where(wide == iota((elements, elements + 2 * margin), 0) + margin, -4.0, 0.0)
    for k in range(neigh_ref.shape[1]):
        weights = weights + jnp.where(wide == ids[:, k:k + 1], 1.0, 0.0)
    spread_gap = iota((cols, elements), 0) - 9 * iota((cols, elements), 1)
    spread = ones_where((spread_gap >= 0) & (spread_gap < 9), F32)

    up.wait()
    down.wait()
    change = 0.2 * exact(weights, ext[...])
    state = gcm + exact(spread, change)
    dyn[...] = state

    payload = jnp.concatenate(
        [state.astype(BF16), jnp.broadcast_to(substeps_ref[...].astype(F32), (cols, width)).astype(BF16)],
        axis=1)
    fsend[...] = fast(scatter, payload).astype(BF16).reshape(n, capp, 2 * width)

    def forcing_copy(k):
        return pltpu.make_async_remote_copy(
            src_ref=fsend.at[lax.rem(me + k, n)], dst_ref=frecv.at[me],
            send_sem=f_send.at[k], recv_sem=f_recv.at[k],
            device_id={"col": lax.rem(me + k, n)}, device_id_type=MESH)

    def start(copy):
        def body(k, carry):
            copy(k).start()
            return carry
        lax.fori_loop(1, n, body, 0)

    def wait_recv(copy):
        def body(k, carry):
            copy(k).wait_recv()
            return carry
        lax.fori_loop(1, n, body, 0)

    def wait_send(copy):
        def body(k, carry):
            copy(k).wait_send()
            return carry
        lax.fori_loop(1, n, body, 0)

    start(forcing_copy)
    frecv[me] = fsend[me]

    left, right, total = step_matrices(across, width)
    p_lane = iota((slots, table), 1)
    q_lane = (p_lane >> shift) * cap + (p_lane & (capp - 1))
    compact = ones_where((q_lane == iota((slots, table), 0)) & ((p_lane & (capp - 1)) < cap))

    wait_recv(forcing_copy)
    fc[...] = fast(compact, frecv[...].reshape(table, 2 * width))

    def chunk(c, carry):
        at = pl.multiple_of(c * GROUP, GROUP)
        rows = pl.ds(at, GROUP)
        forcing = fc[rows, 0:width]
        count = fc[rows, width:2 * width]
        begin = cloud_ref[rows].reshape(GROUP * across, width)
        lanes = jnp.broadcast_to(count[:, None, :], (GROUP, across, width))
        lanes = lanes.reshape(GROUP * across, width)
        first = one_step(begin, forcing, left, right, across, width)
        first = jnp.where(lanes > 0.5, first, begin.astype(F32)).astype(BF16)
        second = one_step(first, forcing, left, right, across, width)
        second = jnp.where(lanes > 1.5, second, first.astype(F32))
        final = second.astype(BF16)
        gain = fast(total, final) - fast(total, begin)
        tend[rows, :] = gain * (1.0 / across) / jnp.maximum(count, 1.0)
        after[rows] = final.reshape(GROUP, across, width)
        stay = jnp.broadcast_to(keep[rows, :][:, None, :], (GROUP, across, width))
        crm_ref[rows] = (second.reshape(GROUP, across, width) * stay).astype(BF16)
        return carry

    lax.fori_loop(0, slots // GROUP, chunk, 0)

    p_row = iota((table, slots), 0)
    q_row = (p_row >> shift) * cap + (p_row & (capp - 1))
    expand = ones_where((q_row == iota((table, slots), 1)) & ((p_row & (capp - 1)) < cap))
    tsend[...] = fast(expand, tend[...].astype(BF16)).astype(BF16).reshape(n, capp, width)

    def tendency_copy(k):
        return pltpu.make_async_remote_copy(
            src_ref=tsend.at[lax.rem(me + k, n)], dst_ref=trecv.at[me],
            send_sem=t_send.at[k], recv_sem=t_recv.at[k],
            device_id={"col": lax.rem(me + k, n)}, device_id_type=MESH)

    start(tendency_copy)
    trecv[me] = tsend[me]

    def pack(dest):
        base = dest * mcap
        for r in range(mcap):
            depart[base + r] = after[pick_ref[base + r]]

    def mig_copy(k):
        dest = lax.rem(me + k, n)
        return pltpu.make_async_remote_copy(
            src_ref=depart.at[pl.ds(dest * mcap, mcap)],
            dst_ref=arrived_ref.at[pl.ds(me * mcap, mcap)],
            send_sem=m_send.at[k], recv_sem=m_recv.at[k],
            device_id={"col": dest}, device_id_type=MESH)

    def depart_body(k, carry):
        pack(lax.rem(me + k, n))
        mig_copy(k).start()
        return carry

    lax.fori_loop(1, n, depart_body, 0)
    pack(me)
    own = pltpu.make_async_copy(
        depart.at[pl.ds(me * mcap, mcap)], arrived_ref.at[pl.ds(me * mcap, mcap)], own_sem)
    own.start()

    owner_col = owner_col_ref[...]
    hits_col = iota((cols, n), 1) == owner_col
    earlier_col = ones_where(iota((cols, cols), 1) < iota((cols, cols), 0))
    before_col = fast(earlier_col, ones_where(hits_col))
    rank_col = jnp.sum(jnp.where(hits_col, before_col, 0.0), axis=1, keepdims=True).astype(I32)
    place_col = owner_col * capp + rank_col
    gather = ones_where(iota((cols, table), 1) == place_col)
    wait_recv(tendency_copy)
    new_ref[...] = dyn[...] + fast(gather, trecv[...].reshape(table, width))

    wait_recv(mig_copy)
    wait_send(forcing_copy)
    wait_send(tendency_copy)
    wait_send(mig_copy)
    own.wait()


def per_device(gcm_state, cloud_model_state, owner, substeps, neighbours, mig_slot, mig_dest):
    n = lax.axis_size("col")
    cols, width = gcm_state.shape
    slots, across, _ = cloud_model_state.shape
    cap = slots // n
    capp = 16
    while capp < cap:
        capp *= 2
    listed = mig_slot.shape[0]
    mcap = max(2, 2 * listed // n)
    elements = cols // 9
    dest = mig_dest[:, 0]
    order = jnp.arange(listed, dtype=I32)
    rank = jnp.sum(((dest[:, None] == dest[None, :]) & (order[None, :] < order[:, None])).astype(I32), axis=1)
    place = dest * mcap + rank
    spots = jnp.arange(n * mcap, dtype=I32)
    pick = jnp.min(jnp.where(place[None, :] == spots[:, None], mig_slot[None, :], slots), axis=1)
    vmem = pl.BlockSpec(memory_space=pltpu.VMEM)
    dma = pltpu.SemaphoreType.DMA
    table = n * capp
    return pl.pallas_call(
        functools.partial(kernel, n, cap, capp, mcap),
        out_shape=(
            jax.ShapeDtypeStruct((cols, width), F32),
            jax.ShapeDtypeStruct((slots, across, width), BF16),
            jax.ShapeDtypeStruct((n * mcap, across, width), BF16),
        ),
        in_specs=[vmem] * 7 + [pl.BlockSpec(memory_space=pltpu.SMEM)],
        out_specs=(vmem, vmem, pl.BlockSpec(memory_space=pl.ANY)),
        scratch_shapes=[
            pltpu.VMEM((2 * elements, width), F32),
            pltpu.VMEM((cols, width), F32),
            pltpu.VMEM((n, capp, 2 * width), BF16),
            pltpu.VMEM((n, capp, 2 * width), BF16),
            pltpu.VMEM((slots, 2 * width), F32),
            pltpu.VMEM((slots, width), F32),
            pltpu.VMEM((slots, width), F32),
            pltpu.VMEM((n, capp, width), BF16),
            pltpu.VMEM((n, capp, width), BF16),
            pltpu.VMEM((slots + 1, across, width), BF16),
            pltpu.VMEM((n * mcap, across, width), BF16),
            dma((2,)), dma((2,)), dma((n,)), dma((n,)), dma((n,)), dma((n,)), dma((n,)), dma((n,)),
            dma,
        ],
        compiler_params=pltpu.CompilerParams(
            collective_id=0, has_side_effects=True, vmem_limit_bytes=40 * 1024 * 1024),
        cost_estimate=pl.CostEstimate(flops=5 * 10**9, bytes_accessed=10**7, transcendentals=2 * 10**6),
    )(
        gcm_state, cloud_model_state, owner, owner.reshape(1, cols), substeps.reshape(cols, 1),
        neighbours, mig_slot.reshape(1, listed), pick,
    )


def solution(mesh):
    wide, deep, flat = P(("ens", "col"), None), P(("ens", "col"), None, None), P(("ens", "col"))
    return jax.shard_map(
        per_device, mesh=mesh,
        in_specs=(wide, deep, wide, flat, wide, flat, wide),
        out_specs=(wide, deep, deep), check_vma=False,
    )
```

time: 225 us -> 97.1 us (0.43)
  Pallas kernels: 0 us -> 83.9 us
  local copies, waits for them, and re-layouts: 90.8 us -> 9.56 us
  other arithmetic: 59.2 us -> 2.33 us
  waiting for transfers between devices: 45.3 us -> 0 us
  starting transfers between devices: 26.8 us -> 0 us
    pallas_call x0 -> x1, Pallas kernels: none -> 83.9 us  [per_device(): pl.pallas_call(functools.partial(kernel, n, cap, capp, mcap), out_shape=(...]
    all_to_all x4 -> x0, waiting for transfers between devices: 45.3 us -> none  [the longest x1 40.6 us: per_device(): lax.all_to_all(departing, 'col', split_axis=0, concat_axis=0, tiled=True)]
    mul x8 -> x0, local copies, waits for them, and re-layouts: 33.9 us -> none  [the longest x6 21.4 us: crm_steps(): phase[:, :, None, :] * signs]
    mul x7 -> x0, other arithmetic: 24.9 us -> none  [the longest x2 14.4 us: crm_steps(): VERTICAL_RATE * vertical_flux]
    all_to_all x4 -> x0, starting transfers between devices: 24.9 us -> none  [the longest x1 6.64 us: per_device(): lax.all_to_all(send_count_table.astype(jnp.bfloat16), 'col', split_axis=0...]
    scatter x4 -> x0, local copies, waits for them, and re-layouts: 20.2 us -> none  [the longest x1 13.7 us: per_device(): departing = jnp.zeros((device_count * move_cap, across_flux, model_width)...]
    reduce_sum x7 -> x1, other arithmetic: 17.1 us -> 0.9 us  [per_device(): jnp.sum(((dest[:, None] == dest[None, :]) & (order[None, :] < order[:, No...]
    slice x7 -> x0, local copies, waits for them, and re-layouts: 14.7 us -> none  [the longest x4 11.6 us: crm_steps(): jnp.roll(state_field, 1, axis=1) + jnp.roll(state_field, -1, axis=1)]
  transfers between devices with their start and end apart: 6 -> 0, of which waited for: 2 -> 0; matrix products, arithmetic and copies ran while one was open for 35% -> 0% of each run, Pallas kernels for 0% -> 0%
where the time goes in v1:
time: 97.1 us; the launch traced here: 96.5 us
  Pallas kernels  83.9 us (86%)
  local copies, waits for them, and re-layouts  9.56 us (10%)
  other arithmetic  2.33 us (2%)
    pallas_call x1, Pallas kernels, per_device(): pl.pallas_call(functools.partial(kernel, n, cap, capp, mcap), out_shape=(...  83.9 us
    unnamed x13, local copies, waits for them, and re-layouts  8.78 us

profile of v1, /device:TPU:15, one launch (start us, length us, event | category | flops | bytes accessed | tf_op | source)
XLA Modules:
  0.0 96.5 jit_solution(13513042862180412665)
XLA Ops:
  0.6 0.9 convert_reduce_fusion
  1.5 0.7 multiply_add_fusion
  2.2 0.8 select_reduce_fusion.pick_ref
  3.0 0.8 copy.17.neigh_ref
  3.7 0.8 copy.16.substeps_ref
  4.5 0.8 copy.15.owner_col_ref
  5.3 0.0 copy-start
  5.3 0.7 copy-done
  6.0 0.0 copy-start.1
  6.0 0.7 copy-done.1
  6.6 0.0 copy-start.2
  6.6 1.7 %copy-done.2 = bf16[288,32,128]{2,1,0:T(8,128)(2,1)S(1)} copy-done((bf16[288,32,128]{2,1,0:T(8,128)(2,1)S(1)}, bf16[288,32,128]{2,1,0:T(8,128)(2,1)}, u32[]{:S(2)}) %copy-start.2) | copy-done | bytes 2359320
  8.3 0.0 copy-start.3
  8.3 0.9 copy-done.3
  9.2 83.9 %shard_map.94 = (f32[144,128]{1,0:T(8,128)S(1)}, bf16[288,32,128]{2,1,0:T(8,128)(2,1)S(1)}, bf16[256,32,128]{2,1,0:T(8,128)(2,1)S(1)}) custom-call(f32[144,128]{1,0:T(8,128)S(1)} %copy-done.3, bf16[288,32,128]{2,1,0:T(8,128)(2,1)S(1)} %copy-done.2, s32[144,1]{1,0:T(8,128)S(1)} %copy.15.owner_col_ref, s32[1,144]{1,0:T(1,128)S(1)} %bitcast.5, ...), custom_call_target="tpu_custom_call" | custom-call | flops 5000000000 | bytes 10000000 | tf_op jit(solution)/shard_map/pallas_call | solution.py:272
  93.1 0.6 copy.21
  93.8 1.4 %copy.22 = bf16[288,32,128]{2,1,0:T(8,128)(2,1)} copy(bf16[288,32,128]{2,1,0:T(8,128)(2,1)S(1)} %get-tuple-element.7) | data formatting | bytes 4718592
  95.2 1.3 %copy.23 = bf16[256,32,128]{2,1,0:T(8,128)(2,1)} copy(bf16[256,32,128]{2,1,0:T(8,128)(2,1)S(1)} %get-tuple-element.8) | data formatting | bytes 4194304
Async XLA Ops:
  5.3 0.7 copy-start
  6.0 0.7 copy-start.1
  6.6 1.7 %copy-start.2 = (bf16[288,32,128]{2,1,0:T(8,128)(2,1)S(1)}, bf16[288,32,128]{2,1,0:T(8,128)(2,1)}, u32[]{:S(2)}) copy-start(bf16[288,32,128]{2,1,0:T(8,128)(2,1)} %cloud_ref.1) | copy-start | bytes 7077892
  8.3 0.9 copy-start.3

commit v2 on v1

v2 whole, which is shorter than its diff:
```python
import functools

import jax
import jax.numpy as jnp
from jax import lax
from jax.experimental import pallas as pl
from jax.experimental.pallas import tpu as pltpu
from jax.sharding import PartitionSpec as P

F32, BF16, I32 = jnp.float32, jnp.bfloat16, jnp.int32
MESH = pl.DeviceIdType.MESH
GROUP = 8
TOGETHER = 4
BATCH = 16
EARLY = 4


def iota(shape, dim):
    return lax.broadcasted_iota(I32, shape, dim)


def ones_where(condition, dtype=BF16):
    return jnp.where(condition, 1.0, 0.0).astype(dtype)


def exact(a, b):
    return jnp.dot(a, b, preferred_element_type=F32, precision=lax.Precision.HIGHEST)


def fast(a, b):
    return jnp.dot(a, b, preferred_element_type=F32)


def step_matrices(across, width):
    size = GROUP * across
    shift = across.bit_length() - 1
    row, col = iota((size, size), 0), iota((size, size), 1)
    same = (row >> shift) == (col >> shift)
    gap = (row - col) & (across - 1)
    beside = jnp.where((gap == 1) | (gap == across - 1), 1.0, 0.0)
    middle = jnp.where(gap == 0, 3.0, 0.0)
    left = jnp.where(same, beside + middle - 1.5 / across, 0.0).astype(BF16)
    half = width // 2
    source, level = iota((width, 2 * width), 0), iota((width, 2 * width), 1)
    inside = (source < half) == (level < half)
    near = jnp.where(jnp.abs(source - level) == 1, 0.75, 0.0)
    edge = (level == 0) | (level == half - 1) | (level == half) | (level == width - 1)
    near = near - jnp.where(source == level, jnp.where(edge, 0.75, 1.5), 0.0)
    vertical = jnp.where(inside, near, 0.0)
    target = level - width
    sign = jnp.where(target < half, 1.0, -1.0)
    of_level = (source & (half - 1)) == (target & (half - 1))
    phase = jnp.where(of_level, jnp.where(source < half, -0.5, 1.0) * sign, 0.0)
    right = jnp.where(level < width, vertical, phase).astype(BF16)
    rows = iota((GROUP, size), 0)
    total = ones_where(rows == (iota((GROUP, size), 1) >> shift))
    return left, right, total


def steps(states, forcings, counts, left, right, across, width):
    size = GROUP * across
    spread = lambda rows: jnp.broadcast_to(rows[:, None, :], (GROUP, across, width)).reshape(size, width)
    states = list(states)
    for least in (0.5, 1.5):
        linear = [fast(left, state) for state in states]
        levels = [fast(state, right) for state in states]
        moved = [
            0.2 * (a + b[:, :width] + spread(1.5 * f)) + 0.25 * jnp.tanh(b[:, width:])
            for a, b, f in zip(linear, levels, forcings)
        ]
        states = [
            jnp.where(spread(count) > least, new, old.astype(F32)).astype(BF16)
            for new, old, count in zip(moved, states, counts)
        ]
    return states


def kernel(n, cap, capp, mcap,
           gcm_hbm, cloud_hbm, owner_ref, substeps_ref, neigh_ref, slot_ref, dest_ref,
           new_ref, crm_ref, arrived_ref,
           gcm_ref, ext, dyn, fsend, frecv, fc, fbatch, keep, tend, tsend, trecv, work, depart,
           pick_v, pick,
           halo_send, halo_recv, f_send, f_recv, t_send, t_recv, m_send, m_recv, own_sem,
           gcm_sem, cloud_sem, pick_sem):
    me = lax.axis_index("col")
    cols, width = gcm_hbm.shape
    slots, across, _ = cloud_hbm.shape
    listed = slot_ref.shape[1]
    elements = cols // 9
    margin = elements // 2
    table = n * capp
    spots = n * mcap
    shift = capp.bit_length() - 1
    right_dev, left_dev = lax.rem(me + 1, n), lax.rem(me + n - 1, n)

    gcm_copy = pltpu.make_async_copy(gcm_hbm, gcm_ref, gcm_sem)
    gcm_copy.start()
    cloud_copy = pltpu.make_async_copy(cloud_hbm, work.at[pl.ds(0, slots)], cloud_sem)
    cloud_copy.start()
    barrier = pltpu.get_barrier_semaphore()

    def greet(k, carry):
        pl.semaphore_signal(barrier, inc=1, device_id={"col": lax.rem(me + k, n)}, device_id_type=MESH)
        return carry

    lax.fori_loop(1, n, greet, 0)

    gcm_copy.wait()
    gcm = gcm_ref[...]
    place = iota((elements, cols), 1) - 9 * iota((elements, cols), 0)
    member = ones_where((place >= 0) & (place < 9), F32)
    means = exact(member, gcm) * (1.0 / 9.0)
    ext[pl.ds(margin, elements), :] = means
    pl.semaphore_wait(barrier, n - 1)

    up = pltpu.make_async_remote_copy(
        src_ref=ext.at[pl.ds(elements, margin)], dst_ref=ext.at[pl.ds(0, margin)],
        send_sem=halo_send.at[0], recv_sem=halo_recv.at[0],
        device_id={"col": right_dev}, device_id_type=MESH)
    down = pltpu.make_async_remote_copy(
        src_ref=ext.at[pl.ds(margin, margin)], dst_ref=ext.at[pl.ds(margin + elements, margin)],
        send_sem=halo_send.at[1], recv_sem=halo_recv.at[1],
        device_id={"col": left_dev}, device_id_type=MESH)
    up.start()
    down.start()

    owner_row = owner_ref[...]
    hits = iota((n, cols), 0) == owner_row
    earlier = ones_where(iota((cols, cols), 0) < iota((cols, cols), 1))
    before = fast(ones_where(hits), earlier)
    rank = jnp.sum(jnp.where(hits, before, 0.0), axis=0, keepdims=True).astype(I32)
    place_row = owner_row * capp + rank
    scatter = ones_where(iota((table, cols), 0) == place_row)
    substeps = jnp.broadcast_to(substeps_ref[...].astype(F32), (width, cols)).astype(BF16)
    sent_counts = lax.dot_general(scatter, substeps, (((1,), (1,)), ((), ())), preferred_element_type=F32)
    fsend[:, :, width:2 * width] = sent_counts.astype(BF16).reshape(n, capp, width)

    ids = neigh_ref[...] - me * elements + margin
    span = elements * n
    ids = jnp.where(ids < 0, ids + span, ids)
    ids = jnp.where(ids >= span, ids - span, ids)
    tall = iota((elements + 2 * margin, elements), 0)
    weights = jnp.where(tall == iota((elements + 2 * margin, elements), 1) + margin, -4.0, 0.0)
    for k in range(neigh_ref.shape[0]):
        weights = weights + jnp.where(tall == ids[k:k + 1, :], 1.0, 0.0)
    spread_gap = iota((cols, elements), 0) - 9 * iota((cols, elements), 1)
    spread = ones_where((spread_gap >= 0) & (spread_gap < 9), F32)
    per_column = fast(spread.astype(BF16), weights.T.astype(BF16))

    up.wait()
    down.wait()
    state = gcm + 0.2 * exact(per_column, ext[...])
    dyn[...] = state
    fsend[:, :, 0:width] = fast(scatter, state.astype(BF16)).astype(BF16).reshape(n, capp, width)

    def forcing_copy(k):
        return pltpu.make_async_remote_copy(
            src_ref=fsend.at[lax.rem(me + k, n)], dst_ref=frecv.at[me],
            send_sem=f_send.at[k], recv_sem=f_recv.at[k],
            device_id={"col": lax.rem(me + k, n)}, device_id_type=MESH)

    def start(copy):
        def body(k, carry):
            copy(k).start()
            return carry
        lax.fori_loop(1, n, body, 0)

    def wait_recv(copy):
        def body(k, carry):
            copy(k).wait_recv()
            return carry
        lax.fori_loop(1, n, body, 0)

    def wait_send(copy):
        def body(k, carry):
            copy(k).wait_send()
            return carry
        lax.fori_loop(1, n, body, 0)

    start(forcing_copy)
    frecv[me] = fsend[me]

    slot_row, dest_row = slot_ref[...], dest_ref[...]
    slot_col = jnp.broadcast_to(slot_row, (listed, listed)).T
    dest_col = jnp.broadcast_to(dest_row, (listed, listed)).T
    same = (dest_col == dest_row) & (iota((listed, listed), 1) < iota((listed, listed), 0))
    place_mig = dest_col[:, 0:1] * mcap + jnp.sum(jnp.where(same, 1, 0), axis=1, keepdims=True)
    found = iota((listed, spots), 1) == place_mig
    chosen = jnp.sum(jnp.where(found, slot_col[:, 0:1] - slots, 0), axis=0, keepdims=True) + slots
    pick_v[...] = chosen
    pick_copy = pltpu.make_async_copy(pick_v, pick, pick_sem)
    pick_copy.start()
    gone = iota((slots, listed), 0) == slot_row
    gone = jnp.max(jnp.where(gone, 1.0, 0.0), axis=1, keepdims=True)
    keep[...] = jnp.broadcast_to(1.0 - gone, (slots, width))
    work[pl.ds(slots, 1)] = jnp.zeros((1, across, width), BF16)
    fc[pl.ds(slots, 8), :] = jnp.zeros((8, 2 * width), F32)
    left, right, total = step_matrices(across, width)
    p_lane = iota((slots, table), 1)
    q_lane = (p_lane >> shift) * cap + (p_lane & (capp - 1))
    compact = ones_where((q_lane == iota((slots, table), 0)) & ((p_lane & (capp - 1)) < cap))
    pick_copy.wait()
    cloud_copy.wait()

    wait_recv(forcing_copy)
    fc[pl.ds(0, slots), :] = fast(compact, frecv[...].reshape(table, 2 * width))

    def partner(j):
        half = lax.div(j + 1, 2)
        return n // 2 + jnp.where(lax.rem(j, 2) == 1, -half, half)

    def mig_copy(j):
        k = partner(j)
        return pltpu.make_async_remote_copy(
            src_ref=depart.at[pl.ds(j * mcap, mcap)],
            dst_ref=arrived_ref.at[pl.ds(me * mcap, mcap)],
            send_sem=m_send.at[k], recv_sem=m_recv.at[k],
            device_id={"col": lax.rem(me + k, n)}, device_id_type=MESH)

    per_batch = max(1, BATCH // mcap)
    early = EARLY * per_batch
    size = GROUP * across

    def early_body(b, carry):
        for i in range(BATCH):
            j = b * per_batch + i // mcap
            at = pick[0, lax.rem(me + partner(j), n) * mcap + i % mcap]
            depart[b * BATCH + i] = work[at]
            fbatch[i:i + 1, :] = fc[pl.ds(at, 1), :]
        forcings, counts, states = [], [], []
        for g in range(BATCH // GROUP):
            states.append(depart[pl.ds(b * BATCH + g * GROUP, GROUP)].reshape(size, width))
            forcings.append(fbatch[g * GROUP:(g + 1) * GROUP, 0:width])
            counts.append(fbatch[g * GROUP:(g + 1) * GROUP, width:2 * width])
        finals = steps(states, forcings, counts, left, right, across, width)
        for g, final in enumerate(finals):
            depart[pl.ds(b * BATCH + g * GROUP, GROUP)] = final.reshape(GROUP, across, width)
        for j in range(per_batch):
            mig_copy(b * per_batch + j).start()
        return carry

    lax.fori_loop(0, EARLY, early_body, 0)

    def chunk(c, carry):
        rows = [pl.ds(pl.multiple_of((c * TOGETHER + g) * GROUP, GROUP), GROUP) for g in range(TOGETHER)]
        forcings = [fc[row, 0:width] for row in rows]
        counts = [fc[row, width:2 * width] for row in rows]
        stays = [keep[row, :] for row in rows]
        begins = [work[row].reshape(size, width) for row in rows]
        finals = steps(begins, forcings, counts, left, right, across, width)
        gains = [fast(total, final) - fast(total, begin) for final, begin in zip(finals, begins)]
        for row, final, gain, count, stay in zip(rows, finals, gains, counts, stays):
            tend[row, :] = gain * (1.0 / across) / jnp.maximum(count, 1.0)
            work[row] = final.reshape(GROUP, across, width)
            stay = jnp.broadcast_to(stay[:, None, :], (GROUP, across, width)).astype(BF16)
            crm_ref[row] = final.reshape(GROUP, across, width) * stay
        return carry

    lax.fori_loop(0, slots // (GROUP * TOGETHER), chunk, 0)

    p_row = iota((table, slots), 0)
    q_row = (p_row >> shift) * cap + (p_row & (capp - 1))
    expand = ones_where((q_row == iota((table, slots), 1)) & ((p_row & (capp - 1)) < cap))
    tsend[...] = fast(expand, tend[...].astype(BF16)).astype(BF16).reshape(n, capp, width)

    def tendency_copy(k):
        return pltpu.make_async_remote_copy(
            src_ref=tsend.at[lax.rem(me + k, n)], dst_ref=trecv.at[me],
            send_sem=t_send.at[k], recv_sem=t_recv.at[k],
            device_id={"col": lax.rem(me + k, n)}, device_id_type=MESH)

    start(tendency_copy)
    trecv[me] = tsend[me]

    def pack(j, dest):
        for r in range(mcap):
            depart[j * mcap + r] = work[pick[0, dest * mcap + r]]

    def depart_body(j, carry):
        pack(j, lax.rem(me + partner(j), n))
        mig_copy(j).start()
        return carry

    lax.fori_loop(early, n - 1, depart_body, 0)
    pack(n - 1, me)
    own = pltpu.make_async_copy(
        depart.at[pl.ds((n - 1) * mcap, mcap)], arrived_ref.at[pl.ds(me * mcap, mcap)], own_sem)
    own.start()

    wait_recv(tendency_copy)
    back = lax.dot_general(
        scatter, trecv[...].reshape(table, width), (((0,), (0,)), ((), ())), preferred_element_type=F32)
    new_ref[...] = dyn[...] + back

    wait_send(forcing_copy)
    wait_send(tendency_copy)

    def finish(j, carry):
        mig_copy(j).wait()
        return carry

    lax.fori_loop(0, n - 1, finish, 0)
    own.wait()


def per_device(gcm_state, cloud_model_state, owner, substeps, neighbours, mig_slot, mig_dest):
    n = lax.axis_size("col")
    cols, width = gcm_state.shape
    slots, across, _ = cloud_model_state.shape
    cap = slots // n
    capp = 16
    while capp < cap:
        capp *= 2
    listed = mig_slot.shape[0]
    mcap = max(2, 2 * listed // n)
    elements = cols // 9
    vmem = pl.BlockSpec(memory_space=pltpu.VMEM)
    dma = pltpu.SemaphoreType.DMA
    table = n * capp
    return pl.pallas_call(
        functools.partial(kernel, n, cap, capp, mcap),
        out_shape=(
            jax.ShapeDtypeStruct((cols, width), F32),
            jax.ShapeDtypeStruct((slots, across, width), BF16),
            jax.ShapeDtypeStruct((n * mcap, across, width), BF16),
        ),
        in_specs=[pl.BlockSpec(memory_space=pltpu.HBM)] * 2 + [vmem] * 5,
        out_specs=(vmem, vmem, pl.BlockSpec(memory_space=pltpu.HBM)),
        scratch_shapes=[
            pltpu.VMEM((cols, width), F32),
            pltpu.VMEM((2 * elements, width), F32),
            pltpu.VMEM((cols, width), F32),
            pltpu.VMEM((n, capp, 2 * width), BF16),
            pltpu.VMEM((n, capp, 2 * width), BF16),
            pltpu.VMEM((slots + 8, 2 * width), F32),
            pltpu.VMEM((BATCH, 2 * width), F32),
            pltpu.VMEM((slots, width), F32),
            pltpu.VMEM((slots, width), F32),
            pltpu.VMEM((n, capp, width), BF16),
            pltpu.VMEM((n, capp, width), BF16),
            pltpu.VMEM((slots + 1, across, width), BF16),
            pltpu.VMEM((n * mcap, across, width), BF16),
            pltpu.VMEM((1, n * mcap), I32),
            pltpu.SMEM((1, n * mcap), I32),
            dma((2,)), dma((2,)), dma((n,)), dma((n,)), dma((n,)), dma((n,)), dma((n,)), dma((n,)),
            dma, dma, dma, dma,
        ],
        compiler_params=pltpu.CompilerParams(
            collective_id=0, has_side_effects=True, vmem_limit_bytes=40 * 1024 * 1024),
        cost_estimate=pl.CostEstimate(flops=5 * 10**9, bytes_accessed=10**7, transcendentals=2 * 10**6),
    )(
        gcm_state, cloud_model_state, owner.reshape(1, cols), substeps.reshape(1, cols),
        neighbours.T, mig_slot.reshape(1, listed), mig_dest.reshape(1, listed),
    )


def solution(mesh):
    wide, deep, flat = P(("ens", "col"), None), P(("ens", "col"), None, None), P(("ens", "col"))
    return jax.shard_map(
        per_device, mesh=mesh,
        in_specs=(wide, deep, wide, flat, wide, flat, wide),
        out_specs=(wide, deep, deep), check_vma=False,
    )
```

time: 97.1 us -> 75.1 us (0.77)
  Pallas kernels: 83.9 us -> 64 us
  other arithmetic: 2.33 us -> 0 us
    pallas_call x1, Pallas kernels: 83.9 us -> 64 us  [per_device(): pl.pallas_call(functools.partial(kernel, n, cap, capp, mcap), out_shape=(...]
    unnamed x13 -> x17, local copies, waits for them, and re-layouts: 8.78 us -> 9.25 us
where the time goes in v2:
time: 75.1 us; the launch traced here: 73.9 us
  Pallas kernels  64 us (85%)
  local copies, waits for them, and re-layouts  9.25 us (12%)
    pallas_call x1, Pallas kernels, per_device(): pl.pallas_call(functools.partial(kernel, n, cap, capp, mcap), out_shape=(...  64 us
    unnamed x17, local copies, waits for them, and re-layouts  9.25 us

profile of v2, /device:TPU:15, one launch (start us, length us, event | category | flops | bytes accessed | tf_op | source)
XLA Modules:
  0.0 73.9 jit_solution(11545187999794946823)
XLA Ops:
  0.6 0.0 copy-start
  0.6 1.7 %copy-done = bf16[288,32,128]{2,1,0:T(8,128)(2,1)S(1)} copy-done((bf16[288,32,128]{2,1,0:T(8,128)(2,1)S(1)}, bf16[288,32,128]{2,1,0:T(8,128)(2,1)}, u32[]{:S(2)}) %copy-start) | copy-done | bytes 2359320
  2.3 0.0 copy-start.1
  2.3 0.9 %copy-done.1 = f32[144,128]{1,0:T(8,128)S(1)} copy-done((f32[144,128]{1,0:T(8,128)S(1)}, f32[144,128]{1,0:T(8,128)}, u32[]{:S(2)}) %copy-start.1) | copy-done | bytes 73752
  3.2 0.0 copy-start.2
  3.2 0.7 copy-done.2
  3.9 0.0 copy-start.3
  3.9 0.7 copy-done.3
  4.5 0.0 copy-start.4
  4.5 0.7 copy-done.4
  5.2 0.0 copy-start.5
  5.2 0.7 copy-done.5
  5.9 0.0 copy-start.6
  5.9 0.7 copy-done.6
  6.5 64.0 %shard_map.94 = (f32[144,128]{1,0:T(8,128)S(1)}, bf16[288,32,128]{2,1,0:T(8,128)(2,1)S(1)}, bf16[256,32,128]{2,1,0:T(8,128)(2,1)S(1)}) custom-call(f32[144,128]{1,0:T(8,128)S(1)} %copy-done.1, bf16[288,32,128]{2,1,0:T(8,128)(2,1)S(1)} %copy-done, s32[1,144]{1,0:T(1,128)S(1)} %bitcast.6, s32[1,144]{1,0:T(1,128)S(1)} %bitcast.7, s32[4,16]{1,0:T(4,128)S(1)} %bitcast.5, ...), custom_call_target="tpu_custom_call" | custom-call | flops 5000000000 | bytes 10000000 | tf_op jit(solution)/shard_map/pallas_call | solution.py:320
  70.5 0.6 copy.13
  71.1 1.4 %copy.14 = bf16[288,32,128]{2,1,0:T(8,128)(2,1)} copy(bf16[288,32,128]{2,1,0:T(8,128)(2,1)S(1)} %get-tuple-element.7) | data formatting | bytes 4718592
  72.5 1.3 %copy.15 = bf16[256,32,128]{2,1,0:T(8,128)(2,1)} copy(bf16[256,32,128]{2,1,0:T(8,128)(2,1)S(1)} %get-tuple-element.8) | data formatting | bytes 4194304
Async XLA Ops:
  0.6 1.7 %copy-start = (bf16[288,32,128]{2,1,0:T(8,128)(2,1)S(1)}, bf16[288,32,128]{2,1,0:T(8,128)(2,1)}, u32[]{:S(2)}) copy-start(bf16[288,32,128]{2,1,0:T(8,128)(2,1)} %cloud_hbm.1) | copy-start | bytes 7077892
  2.3 0.9 %copy-start.1 = (f32[144,128]{1,0:T(8,128)S(1)}, f32[144,128]{1,0:T(8,128)}, u32[]{:S(2)}) copy-start(f32[144,128]{1,0:T(8,128)} %gcm_hbm.1) | copy-start | bytes 221188
  3.2 0.7 copy-start.2
  3.9 0.7 copy-start.3
  4.5 0.7 copy-start.4
  5.2 0.7 copy-start.5
  5.9 0.7 copy-start.6

commit v3 on v2

--- a/solution.py
+++ b/solution.py
@@ -12,7 +12,9 @@
 GROUP = 8
 TOGETHER = 4
 BATCH = 16
-EARLY = 4
+EARLY = 3
+PIECES = 2
+RAW = 2
 
 
 def iota(shape, dim):
@@ -76,16 +78,17 @@
 
 
 def kernel(n, cap, capp, mcap,
-           gcm_hbm, cloud_hbm, owner_ref, substeps_ref, neigh_ref, slot_ref, dest_ref,
-           new_ref, crm_ref, arrived_ref,
-           gcm_ref, ext, dyn, fsend, frecv, fc, fbatch, keep, tend, tsend, trecv, work, depart,
-           pick_v, pick,
+           gcm_hbm, cloud_hbm, owner_hbm, substeps_hbm, neigh_hbm, slot_hbm, dest_hbm,
+           new_hbm, crm_hbm, arrived_ref,
+           gcm_ref, owner_ref, substeps_ref, neigh_ref, slot_ref, dest_ref, new_ref, crm_ref, ext, dyn, fsend, frecv, fc, fbatch, keep, tend, tsend, trecv, work, depart,
+           landed, notes, noted, pick_v, pick,
            halo_send, halo_recv, f_send, f_recv, t_send, t_recv, m_send, m_recv, own_sem,
-           gcm_sem, cloud_sem, pick_sem):
+           in_sem, cloud_sem, pick_sem, out_sem,
+           r_send, r_recv, g_send, g_recv, l_sem):
     me = lax.axis_index("col")
     cols, width = gcm_hbm.shape
     slots, across, _ = cloud_hbm.shape
-    listed = slot_ref.shape[1]
+    listed = slot_hbm.shape[1]
     elements = cols // 9
     margin = elements // 2
     table = n * capp
@@ -93,8 +96,14 @@
     shift = capp.bit_length() - 1
     right_dev, left_dev = lax.rem(me + 1, n), lax.rem(me + n - 1, n)
 
-    gcm_copy = pltpu.make_async_copy(gcm_hbm, gcm_ref, gcm_sem)
-    gcm_copy.start()
+    inputs = [
+        pltpu.make_async_copy(source, target, in_sem.at[i])
+        for i, (source, target) in enumerate([
+            (gcm_hbm, gcm_ref), (owner_hbm, owner_ref), (substeps_hbm, substeps_ref),
+            (neigh_hbm, neigh_ref), (slot_hbm, slot_ref), (dest_hbm, dest_ref)])
+    ]
+    for copy in inputs:
+        copy.start()
     cloud_copy = pltpu.make_async_copy(cloud_hbm, work.at[pl.ds(0, slots)], cloud_sem)
     cloud_copy.start()
     barrier = pltpu.get_barrier_semaphore()
@@ -105,7 +114,8 @@
 
     lax.fori_loop(1, n, greet, 0)
 
-    gcm_copy.wait()
+    for copy in inputs:
+        copy.wait()
     gcm = gcm_ref[...]
     place = iota((elements, cols), 1) - 9 * iota((elements, cols), 0)
     member = ones_where((place >= 0) & (place < 9), F32)
@@ -124,6 +134,52 @@
     up.start()
     down.start()
 
+    slot_row, dest_row = slot_ref[...], dest_ref[...]
+    slot_col = jnp.broadcast_to(slot_row, (listed, listed)).T
+    dest_col = jnp.broadcast_to(dest_row, (listed, listed)).T
+    same = (dest_col == dest_row) & (iota((listed, listed), 1) < iota((listed, listed), 0))
+    place_mig = dest_col[:, 0:1] * mcap + jnp.sum(jnp.where(same, 1, 0), axis=1, keepdims=True)
+    found = iota((listed, spots), 1) == place_mig
+    chosen = jnp.sum(jnp.where(found, slot_col[:, 0:1] - slots, 0), axis=0, keepdims=True) + slots
+    pick_v[...] = chosen
+    pick_copy = pltpu.make_async_copy(pick_v, pick, pick_sem)
+    pick_copy.start()
+    work[pl.ds(slots, 1)] = jnp.zeros((1, across, width), BF16)
+    pick_copy.wait()
+    cloud_copy.wait()
+
+    def partner(j):
+        half = lax.div(j + 1, 2)
+        return n // 2 + jnp.where(lax.rem(j, 2) == 1, -half, half)
+
+    def mig_copy(j):
+        k = partner(j)
+        return pltpu.make_async_remote_copy(
+            src_ref=depart.at[pl.ds(j * mcap, mcap)],
+            dst_ref=arrived_ref.at[pl.ds(me * mcap, mcap)],
+            send_sem=m_send.at[k], recv_sem=m_recv.at[k],
+            device_id={"col": lax.rem(me + k, n)}, device_id_type=MESH)
+
+    per_batch = max(1, BATCH // mcap)
+    raw = RAW * per_batch
+
+    def raw_copy(j):
+        return pltpu.make_async_remote_copy(
+            src_ref=depart.at[pl.ds(j * mcap, mcap)], dst_ref=landed.at[pl.ds(j * mcap, mcap)],
+            send_sem=r_send.at[j], recv_sem=r_recv.at[j],
+            device_id={"col": lax.rem(me + partner(j), n)}, device_id_type=MESH)
+
+    def pack(j, dest):
+        for r in range(mcap):
+            depart[j * mcap + r] = work[pick[0, dest * mcap + r]]
+
+    def raw_body(j, carry):
+        pack(j, lax.rem(me + partner(j), n))
+        raw_copy(j).start()
+        return carry
+
+    lax.fori_loop(0, raw // 2, raw_body, 0)
+
     owner_row = owner_ref[...]
     hits = iota((n, cols), 0) == owner_row
     earlier = ones_where(iota((cols, cols), 0) < iota((cols, cols), 1))
@@ -131,9 +187,11 @@
     rank = jnp.sum(jnp.where(hits, before, 0.0), axis=0, keepdims=True).astype(I32)
     place_row = owner_row * capp + rank
     scatter = ones_where(iota((table, cols), 0) == place_row)
-    substeps = jnp.broadcast_to(substeps_ref[...].astype(F32), (width, cols)).astype(BF16)
-    sent_counts = lax.dot_general(scatter, substeps, (((1,), (1,)), ((), ())), preferred_element_type=F32)
-    fsend[:, :, width:2 * width] = sent_counts.astype(BF16).reshape(n, capp, width)
+    p_col = iota((table, cols), 0)
+    count_row = ones_where(((p_col & (capp - 1)) == cap) & ((p_col >> shift) == owner_row))
+    count_lane = jnp.where(iota((width, cols), 0) == rank, substeps_ref[...].astype(F32), 0.0).astype(BF16)
+    sent_counts = lax.dot_general(count_row, count_lane, (((1,), (1,)), ((), ())), preferred_element_type=F32)
+    fsend[...] = sent_counts.astype(BF16).reshape(n, capp, width)
 
     ids = neigh_ref[...] - me * elements + margin
     span = elements * n
@@ -151,7 +209,8 @@
     down.wait()
     state = gcm + 0.2 * exact(per_column, ext[...])
     dyn[...] = state
-    fsend[:, :, 0:width] = fast(scatter, state.astype(BF16)).astype(BF16).reshape(n, capp, width)
+    sent = fast(scatter, state.astype(BF16)) + fsend[...].reshape(table, width).astype(F32)
+    fsend[...] = sent.astype(BF16).reshape(n, capp, width)
 
     def forcing_copy(k):
         return pltpu.make_async_remote_copy(
@@ -178,48 +237,54 @@
         lax.fori_loop(1, n, body, 0)
 
     start(forcing_copy)
+    lax.fori_loop(raw // 2, raw, raw_body, 0)
     frecv[me] = fsend[me]
 
-    slot_row, dest_row = slot_ref[...], dest_ref[...]
-    slot_col = jnp.broadcast_to(slot_row, (listed, listed)).T
-    dest_col = jnp.broadcast_to(dest_row, (listed, listed)).T
-    same = (dest_col == dest_row) & (iota((listed, listed), 1) < iota((listed, listed), 0))
-    place_mig = dest_col[:, 0:1] * mcap + jnp.sum(jnp.where(same, 1, 0), axis=1, keepdims=True)
-    found = iota((listed, spots), 1) == place_mig
-    chosen = jnp.sum(jnp.where(found, slot_col[:, 0:1] - slots, 0), axis=0, keepdims=True) + slots
-    pick_v[...] = chosen
-    pick_copy = pltpu.make_async_copy(pick_v, pick, pick_sem)
-    pick_copy.start()
-    gone = iota((slots, listed), 0) == slot_row
+    gone = iota((slots, listed), 0) == slot_ref[...]
     gone = jnp.max(jnp.where(gone, 1.0, 0.0), axis=1, keepdims=True)
     keep[...] = jnp.broadcast_to(1.0 - gone, (slots, width))
-    work[pl.ds(slots, 1)] = jnp.zeros((1, across, width), BF16)
     fc[pl.ds(slots, 8), :] = jnp.zeros((8, 2 * width), F32)
     left, right, total = step_matrices(across, width)
     p_lane = iota((slots, table), 1)
     q_lane = (p_lane >> shift) * cap + (p_lane & (capp - 1))
     compact = ones_where((q_lane == iota((slots, table), 0)) & ((p_lane & (capp - 1)) < cap))
-    pick_copy.wait()
-    cloud_copy.wait()
+    first = (p_lane >> shift) * cap
+    q_table = iota((slots, table), 0)
+    counting = ones_where(((p_lane & (capp - 1)) == cap) & (q_table >= first) & (q_table < first + cap))
+    within = fast(compact, ones_where((iota((table, width), 0) & (capp - 1)) == iota((table, width), 1)))
 
     wait_recv(forcing_copy)
-    fc[pl.ds(0, slots), :] = fast(compact, frecv[...].reshape(table, 2 * width))
-
-    def partner(j):
-        half = lax.div(j + 1, 2)
-        return n // 2 + jnp.where(lax.rem(j, 2) == 1, -half, half)
-
-    def mig_copy(j):
-        k = partner(j)
+    received = frecv[...].reshape(table, width)
+    fc[pl.ds(0, slots), 0:width] = fast(compact, received)
+    count = jnp.sum(fast(counting, received) * within, axis=1, keepdims=True)
+    fc[pl.ds(0, slots), width:2 * width] = jnp.broadcast_to(count, (slots, width))
+
+    early = (RAW + EARLY) * per_batch
+    size = GROUP * across
+
+    def note_copy(j):
         return pltpu.make_async_remote_copy(
-            src_ref=depart.at[pl.ds(j * mcap, mcap)],
-            dst_ref=arrived_ref.at[pl.ds(me * mcap, mcap)],
-            send_sem=m_send.at[k], recv_sem=m_recv.at[k],
-            device_id={"col": lax.rem(me + k, n)}, device_id_type=MESH)
-
-    per_batch = max(1, BATCH // mcap)
-    early = EARLY * per_batch
-    size = GROUP * across
+            src_ref=notes.at[j], dst_ref=noted.at[j],
+            send_sem=g_send.at[j], recv_sem=g_recv.at[j],
+            device_id={"col": lax.rem(me + partner(j), n)}, device_id_type=MESH)
+
+    def note_body(b, carry):
+        for i in range(BATCH):
+            j = b * per_batch + i // mcap
+            at = pick[0, lax.rem(me + partner(j), n) * mcap + i % mcap]
+            fbatch[i:i + 1, :] = fc[pl.ds(at, 1), :]
+        forcing, count = fbatch[:, 0:width], fbatch[:, width:2 * width]
+        row, lane = iota((BATCH, width), 0), iota((BATCH, width), 1)
+        for g in range(per_batch):
+            mine = (row >= g * mcap) & (row < (g + 1) * mcap)
+            line = jnp.sum(jnp.where(mine & (row == lane), count, 0.0), axis=0, keepdims=True)
+            lower = jnp.where(row == 0, jnp.broadcast_to(line, (BATCH, width)), 0.0)
+            notes[b * per_batch + g] = jnp.concatenate(
+                [jnp.where(mine, forcing, 0.0), lower], axis=0).astype(BF16)
+            note_copy(b * per_batch + g).start()
+        return carry
+
+    lax.fori_loop(0, RAW, note_body, 0)
 
     def early_body(b, carry):
         for i in range(BATCH):
@@ -239,7 +304,7 @@
             mig_copy(b * per_batch + j).start()
         return carry
 
-    lax.fori_loop(0, EARLY, early_body, 0)
+    lax.fori_loop(RAW, RAW + EARLY, early_body, 0)
 
     def chunk(c, carry):
         rows = [pl.ds(pl.multiple_of((c * TOGETHER + g) * GROUP, GROUP), GROUP) for g in range(TOGETHER)]
@@ -272,10 +337,6 @@
     start(tendency_copy)
     trecv[me] = tsend[me]
 
-    def pack(j, dest):
-        for r in range(mcap):
-            depart[j * mcap + r] = work[pick[0, dest * mcap + r]]
-
     def depart_body(j, carry):
         pack(j, lax.rem(me + partner(j), n))
         mig_copy(j).start()
@@ -287,10 +348,42 @@
         depart.at[pl.ds((n - 1) * mcap, mcap)], arrived_ref.at[pl.ds(me * mcap, mcap)], own_sem)
     own.start()
 
+    def landed_copy(j):
+        source = lax.rem(me - partner(j) + n, n)
+        return pltpu.make_async_copy(
+            landed.at[pl.ds(j * mcap, mcap)], arrived_ref.at[pl.ds(source * mcap, mcap)], l_sem.at[j])
+
+    def landed_body(b, carry):
+        note = jnp.zeros((2 * BATCH, width), F32)
+        for g in range(per_batch):
+            raw_copy(b * per_batch + g).wait_recv()
+            note_copy(b * per_batch + g).wait_recv()
+            note = note + noted[b * per_batch + g].astype(F32)
+        row, lane = iota((BATCH, width), 0), iota((BATCH, width), 1)
+        line = jnp.broadcast_to(note[BATCH:BATCH + 1, :], (BATCH, width))
+        count = jnp.sum(jnp.where(row == lane, line, 0.0), axis=1, keepdims=True)
+        count = jnp.broadcast_to(count, (BATCH, width))
+        parts = [slice(g * GROUP, (g + 1) * GROUP) for g in range(BATCH // GROUP)]
+        places = [pl.ds(b * BATCH + g * GROUP, GROUP) for g in range(BATCH // GROUP)]
+        finals = steps(
+            [landed[at].reshape(size, width) for at in places], [note[part] for part in parts],
+            [count[part] for part in parts], left, right, across, width)
+        for at, final in zip(places, finals):
+            landed[at] = final.reshape(GROUP, across, width)
+        for g in range(per_batch):
+            landed_copy(b * per_batch + g).start()
+        return carry
+
+    lax.fori_loop(0, RAW, landed_body, 0)
+
+    crm_copy = pltpu.make_async_copy(crm_ref, crm_hbm, out_sem.at[0])
+    crm_copy.start()
     wait_recv(tendency_copy)
     back = lax.dot_general(
         scatter, trecv[...].reshape(table, width), (((0,), (0,)), ((), ())), preferred_element_type=F32)
     new_ref[...] = dyn[...] + back
+    new_copy = pltpu.make_async_copy(new_ref, new_hbm, out_sem.at[1])
+    new_copy.start()
 
     wait_send(forcing_copy)
     wait_send(tendency_copy)
@@ -299,8 +392,39 @@
         mig_copy(j).wait()
         return carry
 
-    lax.fori_loop(0, n - 1, finish, 0)
+    lax.fori_loop(raw, n - 1, finish, 0)
+
+    def finish_raw(j, carry):
+        raw_copy(j).wait_send()
+        note_copy(j).wait_send()
+        landed_copy(j).wait()
+        return carry
+
+    lax.fori_loop(0, raw, finish_raw, 0)
     own.wait()
+    crm_copy.wait()
+    new_copy.wait()
+
+
+def store(*refs):
+    count = (len(refs) - 2) // 3
+    sources, targets, stages = refs[:count], refs[count:2 * count], refs[2 * count:3 * count]
+    sems_in, sems_out = refs[-2:]
+    reads, writes = [], []
+    for source, target, stage in zip(sources, targets, stages):
+        parts = 1 if len(source.shape) == 2 else PIECES
+        rows = source.shape[0] // parts
+        for i in range(parts):
+            at, sem = pl.ds(i * rows, rows), len(reads)
+            reads.append(pltpu.make_async_copy(source.at[at], stage.at[at], sems_in.at[sem]))
+            writes.append(pltpu.make_async_copy(stage.at[at], target.at[at], sems_out.at[sem]))
+    for read in reads:
+        read.start()
+    for read, write in zip(reads, writes):
+        read.wait()
+        write.start()
+    for write in writes:
+        write.wait()
 
 
 def per_device(gcm_state, cloud_model_state, owner, substeps, neighbours, mig_slot, mig_dest):
@@ -309,29 +433,38 @@
     slots, across, _ = cloud_model_state.shape
     cap = slots // n
     capp = 16
-    while capp < cap:
+    while capp <= cap:
         capp *= 2
     listed = mig_slot.shape[0]
     mcap = max(2, 2 * listed // n)
     elements = cols // 9
-    vmem = pl.BlockSpec(memory_space=pltpu.VMEM)
+    hbm = pl.BlockSpec(memory_space=pltpu.HBM)
+    anywhere = pl.BlockSpec(memory_space=pl.ANY)
     dma = pltpu.SemaphoreType.DMA
     table = n * capp
-    return pl.pallas_call(
+    raw = RAW * max(1, BATCH // mcap)
+    results = pl.pallas_call(
         functools.partial(kernel, n, cap, capp, mcap),
         out_shape=(
             jax.ShapeDtypeStruct((cols, width), F32),
             jax.ShapeDtypeStruct((slots, across, width), BF16),
             jax.ShapeDtypeStruct((n * mcap, across, width), BF16),
         ),
-        in_specs=[pl.BlockSpec(memory_space=pltpu.HBM)] * 2 + [vmem] * 5,
-        out_specs=(vmem, vmem, pl.BlockSpec(memory_space=pltpu.HBM)),
+        in_specs=[hbm] * 7,
+        out_specs=(hbm, hbm, hbm),
         scratch_shapes=[
             pltpu.VMEM((cols, width), F32),
+            pltpu.VMEM((1, cols), I32),
+            pltpu.VMEM((1, cols), I32),
+            pltpu.VMEM(neighbours.shape[::-1], I32),
+            pltpu.VMEM((1, listed), I32),
+            pltpu.VMEM((1, listed), I32),
+            pltpu.VMEM((cols, width), F32),
+            pltpu.VMEM((slots, across, width), BF16),
             pltpu.VMEM((2 * elements, width), F32),
             pltpu.VMEM((cols, width), F32),
-            pltpu.VMEM((n, capp, 2 * width), BF16),
-            pltpu.VMEM((n, capp, 2 * width), BF16),
+            pltpu.VMEM((n, capp, width), BF16),
+            pltpu.VMEM((n, capp, width), BF16),
             pltpu.VMEM((slots + 8, 2 * width), F32),
             pltpu.VMEM((BATCH, 2 * width), F32),
             pltpu.VMEM((slots, width), F32),
@@ -340,18 +473,29 @@
             pltpu.VMEM((n, capp, width), BF16),
             pltpu.VMEM((slots + 1, across, width), BF16),
             pltpu.VMEM((n * mcap, across, width), BF16),
+            pltpu.VMEM((raw * mcap, across, width), BF16),
+            pltpu.VMEM((raw, 2 * BATCH, width), BF16),
+            pltpu.VMEM((raw, 2 * BATCH, width), BF16),
             pltpu.VMEM((1, n * mcap), I32),
             pltpu.SMEM((1, n * mcap), I32),
             dma((2,)), dma((2,)), dma((n,)), dma((n,)), dma((n,)), dma((n,)), dma((n,)), dma((n,)),
-            dma, dma, dma, dma,
+            dma, dma((6,)), dma, dma, dma((2,)),
+            dma((raw,)), dma((raw,)), dma((raw,)), dma((raw,)), dma((raw,)),
         ],
         compiler_params=pltpu.CompilerParams(
-            collective_id=0, has_side_effects=True, vmem_limit_bytes=40 * 1024 * 1024),
+            collective_id=0, has_side_effects=True, vmem_limit_bytes=56 * 1024 * 1024),
         cost_estimate=pl.CostEstimate(flops=5 * 10**9, bytes_accessed=10**7, transcendentals=2 * 10**6),
     )(
         gcm_state, cloud_model_state, owner.reshape(1, cols), substeps.reshape(1, cols),
         neighbours.T, mig_slot.reshape(1, listed), mig_dest.reshape(1, listed),
     )
+    return pl.pallas_call(
+        store,
+        out_shape=tuple(jax.ShapeDtypeStruct(r.shape, r.dtype) for r in results),
+        in_specs=[anywhere] * 3, out_specs=(anywhere,) * 3,
+        scratch_shapes=[pltpu.VMEM(r.shape, r.dtype) for r in results] + [dma((1 + 2 * PIECES,))] * 2,
+        compiler_params=pltpu.CompilerParams(vmem_limit_bytes=56 * 1024 * 1024),
+    )(*results)
 
 
 def solution(mesh):

time: 75.1 us -> 64.1 us (0.85); the launches traced: 73.9 us -> 63.9 us
  local copies, waits for them, and re-layouts: 9.25 us -> 0 us
    unnamed x17 -> x0, local copies, waits for them, and re-layouts: 9.25 us -> none
    pallas_call x1, Pallas kernels: 64 us -> 59.7 us  [per_device(): pl.pallas_call(functools.partial(kernel, n, cap, capp, mcap), out_shape=(...]
    pallas_call x0 -> x1, Pallas kernels: none -> 3.57 us  [per_device(): pl.pallas_call(store, out_shape=tuple((jax.ShapeDtypeStruct(r.shape, r.dt...]
where the time goes in v3:
time: 64.1 us; the launch traced here: 63.9 us
  Pallas kernels  63.3 us (99%)
    pallas_call x1, Pallas kernels, per_device(): pl.pallas_call(functools.partial(kernel, n, cap, capp, mcap), out_shape=(...  59.7 us
    pallas_call x1, Pallas kernels, per_device(): pl.pallas_call(store, out_shape=tuple((jax.ShapeDtypeStruct(r.shape, r.dt...  3.57 us

profile of v3, /device:TPU:15, one launch (start us, length us, event | category | flops | bytes accessed | tf_op | source)
XLA Modules:
  0.0 63.9 jit_solution(2540663750732526936)
XLA Ops:
  0.6 59.7 %shard_map.94 = (f32[144,128]{1,0:T(8,128)}, bf16[288,32,128]{2,1,0:T(8,128)(2,1)}, bf16[256,32,128]{2,1,0:T(8,128)(2,1)}) custom-call(f32[144,128]{1,0:T(8,128)} %gcm_hbm.1, bf16[288,32,128]{2,1,0:T(8,128)(2,1)} %cloud_hbm.1, s32[1,144]{1,0:T(1,128)} %bitcast.6, s32[1,144]{1,0:T(1,128)} %bitcast.7, s32[4,16]{1,0:T(4,128)} %bitcast.5, s32[1,128]{1,0:T(1,128)} %bitcast.8, ...), custom_call_target="tpu_custom_call" | custom-call | flops 5000000000 | bytes 10000000 | tf_op jit(solution)/shard_map/pallas_call | solution.py:446
  60.4 3.6 %shard_map.95 = (f32[144,128]{1,0:T(8,128)}, bf16[288,32,128]{2,1,0:T(8,128)(2,1)}, bf16[256,32,128]{2,1,0:T(8,128)(2,1)}) custom-call(f32[144,128]{1,0:T(8,128)} %get-tuple-element.6.refs_0_, bf16[288,32,128]{2,1,0:T(8,128)(2,1)} %get-tuple-element.7.refs_1_, bf16[256,32,128]{2,1,0:T(8,128)(2,1)} %get-tuple-element.8.refs_2_), custom_call_target="tpu_custom_call" | custom-call | tf_op jit(solution)/shard_map/pallas_call | solution.py:492

commit v4 on v3

--- a/solution.py
+++ b/solution.py
@@ -121,19 +121,6 @@
     member = ones_where((place >= 0) & (place < 9), F32)
     means = exact(member, gcm) * (1.0 / 9.0)
     ext[pl.ds(margin, elements), :] = means
-    pl.semaphore_wait(barrier, n - 1)
-
-    up = pltpu.make_async_remote_copy(
-        src_ref=ext.at[pl.ds(elements, margin)], dst_ref=ext.at[pl.ds(0, margin)],
-        send_sem=halo_send.at[0], recv_sem=halo_recv.at[0],
-        device_id={"col": right_dev}, device_id_type=MESH)
-    down = pltpu.make_async_remote_copy(
-        src_ref=ext.at[pl.ds(margin, margin)], dst_ref=ext.at[pl.ds(margin + elements, margin)],
-        send_sem=halo_send.at[1], recv_sem=halo_recv.at[1],
-        device_id={"col": left_dev}, device_id_type=MESH)
-    up.start()
-    down.start()
-
     slot_row, dest_row = slot_ref[...], dest_ref[...]
     slot_col = jnp.broadcast_to(slot_row, (listed, listed)).T
     dest_col = jnp.broadcast_to(dest_row, (listed, listed)).T
@@ -147,6 +134,18 @@
     work[pl.ds(slots, 1)] = jnp.zeros((1, across, width), BF16)
     pick_copy.wait()
     cloud_copy.wait()
+    pl.semaphore_wait(barrier, n - 1)
+
+    up = pltpu.make_async_remote_copy(
+        src_ref=ext.at[pl.ds(elements, margin)], dst_ref=ext.at[pl.ds(0, margin)],
+        send_sem=halo_send.at[0], recv_sem=halo_recv.at[0],
+        device_id={"col": right_dev}, device_id_type=MESH)
+    down = pltpu.make_async_remote_copy(
+        src_ref=ext.at[pl.ds(margin, margin)], dst_ref=ext.at[pl.ds(margin + elements, margin)],
+        send_sem=halo_send.at[1], recv_sem=halo_recv.at[1],
+        device_id={"col": left_dev}, device_id_type=MESH)
+    up.start()
+    down.start()
 
     def partner(j):
         half = lax.div(j + 1, 2)

time: 64.1 us -> 63.2 us (0.986)
  Pallas kernels: 63.3 us -> 62.4 us
    pallas_call x1, Pallas kernels: 59.7 us -> 58.9 us  [per_device(): pl.pallas_call(functools.partial(kernel, n, cap, capp, mcap), out_shape=(...]
where the time goes in v4:
time: 63.2 us; the launch traced here: 63.1 us
  Pallas kernels  62.4 us (99%)
  between operations  0.64 us (1%)
    pallas_call x1, Pallas kernels, per_device(): pl.pallas_call(functools.partial(kernel, n, cap, capp, mcap), out_shape=(...  58.9 us
    pallas_call x1, Pallas kernels, per_device(): pl.pallas_call(store, out_shape=tuple((jax.ShapeDtypeStruct(r.shape, r.dt...  3.57 us

profile of v4, /device:TPU:15, one launch (start us, length us, event | category | flops | bytes accessed | tf_op | source)
XLA Modules:
  0.0 63.1 jit_solution(13268285739974296722)
XLA Ops:
  0.6 58.9 %shard_map.94 = (f32[144,128]{1,0:T(8,128)}, bf16[288,32,128]{2,1,0:T(8,128)(2,1)}, bf16[256,32,128]{2,1,0:T(8,128)(2,1)}) custom-call(f32[144,128]{1,0:T(8,128)} %gcm_hbm.1, bf16[288,32,128]{2,1,0:T(8,128)(2,1)} %cloud_hbm.1, s32[1,144]{1,0:T(1,128)} %bitcast.6, s32[1,144]{1,0:T(1,128)} %bitcast.7, s32[4,16]{1,0:T(4,128)} %bitcast.5, s32[1,128]{1,0:T(1,128)} %bitcast.8, ...), custom_call_target="tpu_custom_call" | custom-call | flops 5000000000 | bytes 10000000 | tf_op jit(solution)/shard_map/pallas_call | solution.py:445
  59.5 3.6 %shard_map.95 = (f32[144,128]{1,0:T(8,128)}, bf16[288,32,128]{2,1,0:T(8,128)(2,1)}, bf16[256,32,128]{2,1,0:T(8,128)(2,1)}) custom-call(f32[144,128]{1,0:T(8,128)} %get-tuple-element.6.refs_0_, bf16[288,32,128]{2,1,0:T(8,128)(2,1)} %get-tuple-element.7.refs_1_, bf16[256,32,128]{2,1,0:T(8,128)(2,1)} %get-tuple-element.8.refs_2_), custom_call_target="tpu_custom_call" | custom-call | tf_op jit(solution)/shard_map/pallas_call | solution.py:491

commit v5 on v4

--- a/solution.py
+++ b/solution.py
@@ -96,6 +96,14 @@
     shift = capp.bit_length() - 1
     right_dev, left_dev = lax.rem(me + 1, n), lax.rem(me + n - 1, n)
 
+    barrier = pltpu.get_barrier_semaphore()
+
+    def greet(k, carry):
+        pl.semaphore_signal(barrier, inc=1, device_id={"col": lax.rem(me + k, n)}, device_id_type=MESH)
+        return carry
+
+    lax.fori_loop(1, n, greet, 0)
+
     inputs = [
         pltpu.make_async_copy(source, target, in_sem.at[i])
         for i, (source, target) in enumerate([
@@ -106,14 +114,6 @@
         copy.start()
     cloud_copy = pltpu.make_async_copy(cloud_hbm, work.at[pl.ds(0, slots)], cloud_sem)
     cloud_copy.start()
-    barrier = pltpu.get_barrier_semaphore()
-
-    def greet(k, carry):
-        pl.semaphore_signal(barrier, inc=1, device_id={"col": lax.rem(me + k, n)}, device_id_type=MESH)
-        return carry
-
-    lax.fori_loop(1, n, greet, 0)
-
     for copy in inputs:
         copy.wait()
     gcm = gcm_ref[...]
@@ -133,7 +133,6 @@
     pick_copy.start()
     work[pl.ds(slots, 1)] = jnp.zeros((1, across, width), BF16)
     pick_copy.wait()
-    cloud_copy.wait()
     pl.semaphore_wait(barrier, n - 1)
 
     up = pltpu.make_async_remote_copy(
@@ -177,6 +176,7 @@
         raw_copy(j).start()
         return carry
 
+    cloud_copy.wait()
     lax.fori_loop(0, raw // 2, raw_body, 0)
 
     owner_row = owner_ref[...]

time: 63.2 us -> 63.3 us (level)
  no operation moved by 1% of the time
where the time goes in v5:
time: 63.3 us; the launch traced here: 63.1 us
  Pallas kernels  62.4 us (99%)
  between operations  0.64 us (1%)
    pallas_call x1, Pallas kernels, per_device(): pl.pallas_call(functools.partial(kernel, n, cap, capp, mcap), out_shape=(...  58.9 us
    pallas_call x1, Pallas kernels, per_device(): pl.pallas_call(store, out_shape=tuple((jax.ShapeDtypeStruct(r.shape, r.dt...  3.57 us

profile of v5, /device:TPU:15, one launch (start us, length us, event | category | flops | bytes accessed | tf_op | source)
XLA Modules:
  0.0 63.1 jit_solution(14262198529279381225)
XLA Ops:
  0.6 58.9 %shard_map.94 = (f32[144,128]{1,0:T(8,128)}, bf16[288,32,128]{2,1,0:T(8,128)(2,1)}, bf16[256,32,128]{2,1,0:T(8,128)(2,1)}) custom-call(f32[144,128]{1,0:T(8,128)} %gcm_hbm.1, bf16[288,32,128]{2,1,0:T(8,128)(2,1)} %cloud_hbm.1, s32[1,144]{1,0:T(1,128)} %bitcast.6, s32[1,144]{1,0:T(1,128)} %bitcast.7, s32[4,16]{1,0:T(4,128)} %bitcast.5, s32[1,128]{1,0:T(1,128)} %bitcast.8, ...), custom_call_target="tpu_custom_call" | custom-call | flops 5000000000 | bytes 10000000 | tf_op jit(solution)/shard_map/pallas_call | solution.py:445
  59.5 3.6 %shard_map.95 = (f32[144,128]{1,0:T(8,128)}, bf16[288,32,128]{2,1,0:T(8,128)(2,1)}, bf16[256,32,128]{2,1,0:T(8,128)(2,1)}) custom-call(f32[144,128]{1,0:T(8,128)} %get-tuple-element.6.refs_0_, bf16[288,32,128]{2,1,0:T(8,128)(2,1)} %get-tuple-element.7.refs_1_, bf16[256,32,128]{2,1,0:T(8,128)(2,1)} %get-tuple-element.8.refs_2_), custom_call_target="tpu_custom_call" | custom-call | tf_op jit(solution)/shard_map/pallas_call | solution.py:491
